TPU v7x, 128 devices: a whole 4x4x4 slice. The times are simulated.
128 devices in a mesh: shard: 8 (over x, core), ctx: 4 (over z), tp: 4 (over y).
Axes of the slice: x: 4, y: 4, z: 4, core: 2. Of those that a mesh axis runs over, the one named last changes fastest.
Arguments:
- layer_input: bfloat16 [32768, 1536], P(('shard', 'ctx', 'tp')), may hold values from -4 to 4
- out_cotangent: bfloat16 [32768, 1536], P(('shard', 'ctx', 'tp')), may hold values from -4 to 4
- seq_lengths: int32 [8, 4], P('shard'), may hold values from 1 to 3584, as said below
- norm_gain: bfloat16 [1536], P(('shard', 'ctx')), may hold values from 0.5 to 1.5
- proj_gate: bfloat16 [1536, 3072], P(('shard', 'ctx'), 'tp'), may hold values from -0.15625 to 0.15625
- proj_input: bfloat16 [1536, 3072], P(('shard', 'ctx'), 'tp'), may hold values from -0.15625 to 0.15625
- proj_step: bfloat16 [1536, 48], P(('shard', 'ctx'), 'tp'), may hold values from -0.15625 to 0.15625
- proj_state: bfloat16 [1536, 256], P(('shard', 'ctx')), may hold values from -0.15625 to 0.15625
- conv_inner: bfloat16 [4, 48, 64], P(None, 'tp', ('shard', 'ctx')), may hold values from -3 to 3
- conv_inner_bias: bfloat16 [48, 64], P('tp', ('shard', 'ctx')), may hold values from -1 to 1
- conv_state: bfloat16 [4, 256], P(None, ('shard', 'ctx')), may hold values from -3 to 3
- conv_state_bias: bfloat16 [256], P(('shard', 'ctx')), may hold values from -1 to 1
- decay_log: float32 [48], P('tp'), may hold values from -1 to 1
- step_bias: float32 [48], P('tp'), may hold values from -9 to -3
- skip_scale: float32 [48], P('tp'), may hold values from 0.5 to 1.5
- gate_gain: bfloat16 [48, 64], P('tp', ('shard', 'ctx')), may hold values from 0.5 to 1.5
- proj_out: bfloat16 [3072, 1536], P('tp', ('shard', 'ctx')), may hold values from -0.109375 to 0.109375
Outputs:
- layer_output: bfloat16 [32768, 1536], P(('shard', 'ctx', 'tp'))
- input_grad: float32 [32768, 1536], P(('shard', 'ctx', 'tp'))
- grad_norm_gain: float32 [1536], P(('shard', 'ctx', 'tp'))
- grad_proj_gate: float32 [1536, 3072], P(('shard', 'ctx'), 'tp')
- grad_proj_input: float32 [1536, 3072], P(('shard', 'ctx'), 'tp')
- grad_proj_step: float32 [1536, 48], P(('shard', 'ctx'), 'tp')
- grad_proj_state: float32 [1536, 256], P(('shard', 'ctx', 'tp'))
- grad_conv_inner: float32 [4, 48, 64], P(None, 'tp', ('shard', 'ctx'))
- grad_conv_inner_bias: float32 [48, 64], P('tp', ('shard', 'ctx'))
- grad_conv_state: float32 [4, 256], P(None, ('shard', 'ctx', 'tp'))
- grad_conv_state_bias: float32 [256], P(('shard', 'ctx', 'tp'))
- grad_decay_log: float32 [48], P('tp')
- grad_step_bias: float32 [48], P('tp')
- grad_skip_scale: float32 [48], P('tp')
- grad_gate_gain: float32 [48, 64], P('tp', ('shard', 'ctx'))
- grad_proj_out: float32 [3072, 1536], P('tp', ('shard', 'ctx'))
Inputs may be any that keep to these rules, and one draw needn't show every extreme that they name: `seq_lengths`: each row's lengths sum to 4096, and the longest in every row is exactly 3584.
All inputs are finite; a program needn't handle non-finite values.
Results may differ from a plain program's by a relative error of at most 0.013.
Values may be sent and summed in bfloat16 or wider, within the bound.
A program may use at most 320 MiB of HBM per device.

v0:
```python
import jax
import jax.numpy as jnp
from jax import lax
from jax.sharding import PartitionSpec as P

STRETCH = 256


EPS = 1e-05
HIGH = lax.Precision.HIGHEST


def from_behind(value, axis, steps):
    count = lax.axis_size(axis)
    initial, last = (max(0, -steps), min(count, count - steps))
    return lax.ppermute(value, axis, [(source, source + steps) for source in range(initial, last)])


def prefix(x, axis, join, neutral):
    place = lax.axis_index(axis)
    gathered = jax.tree.map(
        lambda a, kind: lax.all_gather(a.astype(kind), axis), x, (jnp.bfloat16, jnp.bfloat16)
    )
    state = jax.tree.map(lambda a, e: jnp.zeros_like(a) + jnp.asarray(e, a.dtype), x, neutral)

    def prefix_one(turn, state):
        return join(
            state,
            jax.tree.map(
                lambda a, own: lax.dynamic_index_in_dim(a, turn, 0, False).astype(own.dtype),
                gathered,
                x,
            ),
        )

    return lax.fori_loop(0, place, prefix_one, state)


def entering(part, axis, combine, identity):
    count = lax.axis_size(axis)
    place = lax.axis_index(axis)
    ahead = count - 1 - place
    gathered = jax.tree.map(lambda a: lax.all_gather(a, axis), part)
    state = jax.tree.map(lambda a, e: jnp.zeros_like(a) + jnp.asarray(e, a.dtype), part, identity)

    def entering_one(turn, state):
        source = count - 1 - turn
        return combine(
            state, jax.tree.map(lambda a: lax.dynamic_index_in_dim(a, source, 0, False), gathered)
        )

    return lax.fori_loop(0, ahead, entering_one, state)


def silu_of(values_in):
    return values_in * jax.nn.sigmoid(values_in)


def grad_dot(grad_rows, weight):
    return lax.dot_general(
        grad_rows, weight, (((1,), (1,)), ((), ())), preferred_element_type=jnp.float32
    )


def weight_dot(left_rows, right_rows):
    return lax.dot_general(
        left_rows, right_rows, (((0,), (0,)), ((), ())), preferred_element_type=jnp.float32
    )


def link_states(earlier, later):
    return (earlier[0] * later[0], later[0][:, None, None] * earlier[1] + later[1])


def conv_piece(padded_in, weights_in, shifts_in, tap_masks):
    tap_count = weights_in.shape[0]
    row_count = padded_in.shape[0] - tap_count + 1
    summed = jnp.zeros((row_count, padded_in.shape[1]), jnp.float32) + shifts_in[None, :]
    for tap_index in range(tap_count):
        summed = (
            summed
            + padded_in[tap_index : tap_index + row_count]
            * weights_in[tap_index][None, :]
            * tap_masks[tap_index][:, None]
        )
    return silu_of(summed)


def block_step(carried_in, pieces, decay_rate):
    state_now, seg_prev = carried_in
    inner_x, basis_b, basis_c, step_size, seg_here = pieces
    cum_rates = jnp.cumsum(step_size * decay_rate[None, :], axis=0)
    block_len = seg_here.shape[0]
    row_index = jnp.arange(block_len)
    keep_mask = (seg_here[:, None] == seg_here[None, :]) & (
        row_index[:, None] >= row_index[None, :]
    )
    pair_mask = keep_mask[:, :, None]
    log_gaps = jnp.where(pair_mask, cum_rates[:, None, :] - cum_rates[None, :, :], 0.0)
    pair_weights = jnp.where(pair_mask, jnp.exp(log_gaps), 0.0) * step_size[None, :, :]
    inner_dot = jnp.einsum("tn,sn->ts", basis_c, basis_b, precision=HIGH)
    scores = inner_dot[:, :, None] * pair_weights
    local_out = jnp.einsum("tsh,shp->thp", scores, inner_x, precision=HIGH)
    live_rows = (seg_here == seg_prev).astype(jnp.float32)
    carry_fade = jnp.exp(cum_rates) * live_rows[:, None]
    carry_out = (
        jnp.einsum("tn,hpn->thp", basis_c, state_now, precision=HIGH) * carry_fade[:, :, None]
    )
    last_seg = seg_here[block_len - 1]
    last_rate = cum_rates[block_len - 1]
    end_weights = (
        jnp.exp(last_rate[None, :] - cum_rates)
        * (seg_here == last_seg).astype(jnp.float32)[:, None]
        * step_size
    )
    fresh_state = jnp.einsum(
        "shp,sn->hpn", inner_x * end_weights[:, :, None], basis_b, precision=HIGH
    )
    kept_state = state_now * (jnp.exp(last_rate) * live_rows[block_len - 1])[:, None, None]
    return ((fresh_state + kept_state, last_seg), local_out + carry_out)


def device_outputs(
    inner_x, basis_b, basis_c, step_size, decay_rate, state_start, seg_here, seg_before
):
    blocks = inner_x.shape[0] // STRETCH
    head_count = inner_x.shape[1]
    head_width = inner_x.shape[2]
    state_dims = basis_b.shape[1]

    def step_fn(carried_in, pieces):
        return block_step(carried_in, pieces, decay_rate)

    _, outputs = lax.scan(
        step_fn,
        (state_start, seg_before),
        (
            inner_x.reshape(blocks, STRETCH, head_count, head_width),
            basis_b.reshape(blocks, STRETCH, state_dims),
            basis_c.reshape(blocks, STRETCH, state_dims),
            step_size.reshape(blocks, STRETCH, head_count),
            seg_here.reshape(blocks, STRETCH),
        ),
    )
    return outputs.reshape(inner_x.shape)


def device_summary(inner_x, basis_b, step_size, decay_rate, seg_here, seg_before):
    cum_rates = jnp.cumsum(step_size * decay_rate[None, :], axis=0)
    last_rate = cum_rates[cum_rates.shape[0] - 1]
    last_seg = seg_here[seg_here.shape[0] - 1]
    end_weights = (
        jnp.exp(last_rate[None, :] - cum_rates)
        * (seg_here == last_seg).astype(jnp.float32)[:, None]
        * step_size
    )
    summary = jnp.einsum("shp,sn->hpn", inner_x * end_weights[:, :, None], basis_b, precision=HIGH)
    carried = jnp.exp(last_rate) * (last_seg == seg_before).astype(jnp.float32)
    return (carried, summary)


def per_device(
    layer_input,
    out_cotangent,
    seq_lengths,
    norm_gain,
    proj_gate,
    proj_input,
    proj_step,
    proj_state,
    conv_inner,
    conv_inner_bias,
    conv_state,
    conv_state_bias,
    decay_log,
    step_bias,
    skip_scale,
    gate_gain,
    proj_out,
):
    tp_count = lax.axis_size("tp")
    share_rows = layer_input.shape[0]
    row_count = share_rows * tp_count
    ctx_place = lax.axis_index("ctx")
    tp_place = lax.axis_index("tp")
    whole_input, whole_cotangent = (
        lax.all_gather(layer_input, "tp", axis=0, tiled=True),
        lax.all_gather(out_cotangent, "tp", axis=0, tiled=True),
    )
    (
        gate_weight,
        input_weight,
        step_weight,
        conv_inner_weight,
        conv_inner_shift,
        gate_gains_raw,
        out_weight,
        state_weight,
        conv_state_weight,
        conv_state_shift,
        norm_gains_raw,
    ) = (
        lax.all_gather(proj_gate, ("shard", "ctx"), axis=0, tiled=True),
        lax.all_gather(proj_input, ("shard", "ctx"), axis=0, tiled=True),
        lax.all_gather(proj_step, ("shard", "ctx"), axis=0, tiled=True),
        lax.all_gather(conv_inner, ("shard", "ctx"), axis=2, tiled=True),
        lax.all_gather(conv_inner_bias, ("shard", "ctx"), axis=1, tiled=True),
        lax.all_gather(gate_gain, ("shard", "ctx"), axis=1, tiled=True),
        lax.all_gather(proj_out, ("shard", "ctx"), axis=1, tiled=True),
        lax.all_gather(proj_state, ("shard", "ctx"), axis=0, tiled=True),
        lax.all_gather(conv_state, ("shard", "ctx"), axis=1, tiled=True),
        lax.all_gather(conv_state_bias, ("shard", "ctx"), axis=0, tiled=True),
        lax.all_gather(norm_gain, ("shard", "ctx"), axis=0, tiled=True),
    )
    inner_cols = input_weight.shape[1]
    head_count = step_weight.shape[1]
    head_width = inner_cols // head_count
    state_dims = state_weight.shape[1] // 2
    tap_count = conv_state_weight.shape[0]
    ends_at = jnp.cumsum(seq_lengths[0])
    first_pos = ctx_place * row_count

    def segment_of(places):
        found_count = jnp.sum((places[:, None] >= ends_at[None, :]).astype(jnp.int32), axis=1)
        return jnp.where(places >= 0, found_count, -1)

    seg_here = segment_of(first_pos + jnp.arange(row_count, dtype=jnp.int32))
    seg_edge = segment_of(first_pos + jnp.arange(1 - tap_count, 0, dtype=jnp.int32))
    seg_before = seg_edge[tap_count - 2]
    seg_all = jnp.concatenate([seg_edge, seg_here])
    tap_masks = jnp.stack(
        [
            (seg_all[tap_index : tap_index + row_count] == seg_here).astype(jnp.float32)
            for tap_index in range(tap_count)
        ]
    )
    input_wide = whole_input.astype(jnp.float32)
    norm_gains = norm_gains_raw.astype(jnp.float32)
    normed = (
        input_wide
        * lax.rsqrt(jnp.mean(input_wide * input_wide, axis=1, keepdims=True) + EPS)
        * norm_gains[None, :]
    ).astype(jnp.bfloat16)
    gate_pre = jnp.dot(normed, gate_weight, preferred_element_type=jnp.float32)
    inner_pre = jnp.dot(normed, input_weight, preferred_element_type=jnp.float32).astype(
        jnp.bfloat16
    )
    state_pre = jnp.dot(normed, state_weight, preferred_element_type=jnp.float32).astype(
        jnp.bfloat16
    )
    step_pre = jnp.dot(normed, step_weight, preferred_element_type=jnp.float32)
    conv_in = lax.optimization_barrier(jnp.concatenate([inner_pre, state_pre], axis=1))
    edge_in = from_behind(conv_in[row_count - (tap_count - 1) :], "ctx", 1)
    extended = jnp.concatenate([edge_in, conv_in], axis=0).astype(jnp.float32)
    conv_weights = jnp.concatenate(
        [conv_inner_weight.reshape(tap_count, inner_cols), conv_state_weight], axis=1
    ).astype(jnp.float32)
    conv_shifts = jnp.concatenate([conv_inner_shift.reshape(inner_cols), conv_state_shift]).astype(
        jnp.float32
    )

    def conv_apply(padded_in, weights_in, shifts_in):
        return conv_piece(padded_in, weights_in, shifts_in, tap_masks)

    conv_post, conv_pull = jax.vjp(conv_apply, extended, conv_weights, conv_shifts)
    rounded = lax.optimization_barrier(conv_post.astype(jnp.bfloat16)).astype(jnp.float32)
    inner_heads = rounded[:, :inner_cols].reshape(row_count, head_count, head_width)
    basis_b = rounded[:, inner_cols : inner_cols + state_dims]
    basis_c = rounded[:, inner_cols + state_dims :]
    decay_rate = -jnp.exp(decay_log)
    step_size = jax.nn.softplus(step_pre + step_bias[None, :])

    def summary_fn(inner_x, basis_in, step_in, rate_in):
        return device_summary(inner_x, basis_in, step_in, rate_in, seg_here, seg_before)

    (carried, summary), summary_pull = jax.vjp(
        summary_fn, inner_heads, basis_b, step_size, decay_rate
    )
    identity = (jnp.ones_like(carried), jnp.zeros_like(summary))
    _, state_start = prefix((carried, summary), "ctx", link_states, identity)

    def output_fn(inner_x, basis_in, basis_out, step_in, rate_in, start_in):
        return device_outputs(
            inner_x, basis_in, basis_out, step_in, rate_in, start_in, seg_here, seg_before
        )

    ssd_out, output_pull = jax.vjp(
        output_fn, inner_heads, basis_b, basis_c, step_size, decay_rate, state_start
    )
    mixed_out = ssd_out + skip_scale[None, :, None] * inner_heads
    mixed_flat = mixed_out.reshape(row_count, inner_cols)
    gate_silu = silu_of(gate_pre)
    gated_rows = mixed_flat * gate_silu
    square_sum = lax.psum(jnp.sum(gated_rows * gated_rows, axis=1), "tp")
    total_inner = inner_cols * tp_count
    gate_scale = lax.rsqrt(square_sum / total_inner + EPS)
    gate_gains = gate_gains_raw.reshape(inner_cols).astype(jnp.float32)
    branch = (gated_rows * gate_scale[:, None] * gate_gains[None, :]).astype(jnp.bfloat16)
    partial_out = jnp.dot(branch, out_weight, preferred_element_type=jnp.float32)
    out_share = lax.psum_scatter(
        partial_out.astype(jnp.bfloat16), "tp", scatter_dimension=0, tiled=True
    ).astype(jnp.float32)
    own_input = layer_input.astype(jnp.float32)
    layer_output = (own_input + out_share).astype(jnp.bfloat16)
    branch_grad = grad_dot(whole_cotangent, out_weight)
    out_weight_grad = weight_dot(branch, whole_cotangent)
    weighted = branch_grad * gate_gains[None, :]
    cross_sum = lax.psum(jnp.sum(gated_rows * weighted, axis=1), "tp")
    scale_cubed = gate_scale * gate_scale * gate_scale
    gated_grad = (
        gate_scale[:, None] * weighted
        - gated_rows * (scale_cubed * cross_sum / total_inner)[:, None]
    )
    gate_gain_grad = jnp.sum(branch_grad * gated_rows * gate_scale[:, None], axis=0)
    gate_sig = jax.nn.sigmoid(gate_pre)
    mixed_grad = (gated_grad * gate_silu).reshape(row_count, head_count, head_width)
    gate_grad = (gated_grad * mixed_flat * gate_sig * (1.0 + gate_pre * (1.0 - gate_sig))).astype(
        jnp.bfloat16
    )
    skip_grad = jnp.sum(mixed_grad * inner_heads, axis=(0, 2))
    x_grad_first, b_grad_first, c_grad, step_grad_first, rate_grad_first, start_grad = output_pull(
        mixed_grad
    )
    _, after_grad = entering((carried, start_grad), "ctx", link_states, identity)
    carried_grad = jnp.sum(after_grad * state_start, axis=(1, 2))
    x_grad_second, b_grad_second, step_grad_second, rate_grad_second = summary_pull(
        (carried_grad, after_grad)
    )
    inner_grad = (mixed_grad * skip_scale[None, :, None] + x_grad_first + x_grad_second).reshape(
        row_count, inner_cols
    )
    post_grad = jnp.concatenate([inner_grad, b_grad_first + b_grad_second, c_grad], axis=1)
    rate_grad = rate_grad_first + rate_grad_second
    step_pre_grad = (step_grad_first + step_grad_second) * jax.nn.sigmoid(
        step_pre + step_bias[None, :]
    )
    extended_grad, conv_weight_grad, conv_shift_grad = conv_pull(post_grad)
    edge_back = from_behind(extended_grad[: tap_count - 1], "ctx", -1)
    conv_in_grad = extended_grad[tap_count - 1 :] + jnp.concatenate(
        [jnp.zeros((row_count - tap_count + 1, extended_grad.shape[1]), jnp.float32), edge_back],
        axis=0,
    )
    inner_in_grad = conv_in_grad[:, :inner_cols].astype(jnp.bfloat16)
    state_in_grad = conv_in_grad[:, inner_cols:]
    step_in_grad = step_pre_grad.astype(jnp.bfloat16)
    normed_grad = (
        grad_dot(gate_grad, gate_weight)
        + grad_dot(inner_in_grad, input_weight)
        + grad_dot(step_in_grad, step_weight)
    )
    gate_weight_grad = weight_dot(normed, gate_grad)
    input_weight_grad = weight_dot(normed, inner_in_grad)
    step_weight_grad = weight_dot(normed, step_in_grad)
    share_grad, share_state_grad = (
        lax.psum_scatter(
            normed_grad.astype(jnp.bfloat16), "tp", scatter_dimension=0, tiled=True
        ).astype(jnp.float32),
        lax.psum_scatter(
            state_in_grad.astype(jnp.bfloat16), "tp", scatter_dimension=0, tiled=True
        ).astype(jnp.float32),
    )
    share_state_low = share_state_grad.astype(jnp.bfloat16)
    share_grad = share_grad + grad_dot(share_state_low, state_weight)
    normed_share = lax.dynamic_slice_in_dim(normed, tp_place * share_rows, share_rows, 0)
    state_weight_grad = weight_dot(normed_share, share_state_low)
    own_scale = lax.rsqrt(jnp.mean(own_input * own_input, axis=1, keepdims=True) + EPS)
    weighted_in = share_grad * norm_gains[None, :]
    input_grad = (
        own_scale * weighted_in
        - own_input
        * (own_scale * own_scale * own_scale)
        * jnp.mean(own_input * weighted_in, axis=1, keepdims=True)
        + out_cotangent.astype(jnp.float32)
    )
    norm_gain_grad = jnp.sum(share_grad * own_input * own_scale, axis=0)
    head_pack = jnp.concatenate([rate_grad * decay_rate, jnp.sum(step_pre_grad, axis=0), skip_grad])
    spread = lax.axis_size("shard") * lax.axis_size("ctx")
    head_rows = jnp.broadcast_to(head_pack[None, :], (spread, head_pack.shape[0]))
    conv_inner_grad = conv_weight_grad[:, :inner_cols].reshape(tap_count, head_count, head_width)
    conv_inner_shift_grad = conv_shift_grad[:inner_cols].reshape(head_count, head_width)
    gate_gain_heads = gate_gain_grad.reshape(head_count, head_width)
    (
        gate_weight_sum,
        input_weight_sum,
        step_weight_sum,
        conv_inner_sum,
        conv_inner_shift_sum,
        gate_gain_sum,
        head_sum,
        out_weight_sum,
    ) = (
        lax.psum_scatter(gate_weight_grad, ("shard", "ctx"), scatter_dimension=0, tiled=True),
        lax.psum_scatter(input_weight_grad, ("shard", "ctx"), scatter_dimension=0, tiled=True),
        lax.psum_scatter(step_weight_grad, ("shard", "ctx"), scatter_dimension=0, tiled=True),
        lax.psum_scatter(conv_inner_grad, ("shard", "ctx"), scatter_dimension=2, tiled=True),
        lax.psum_scatter(conv_inner_shift_grad, ("shard", "ctx"), scatter_dimension=1, tiled=True),
        lax.psum_scatter(gate_gain_heads, ("shard", "ctx"), scatter_dimension=1, tiled=True),
        lax.psum_scatter(head_rows, ("shard", "ctx"), scatter_dimension=0, tiled=True),
        lax.psum_scatter(out_weight_grad, ("shard", "ctx"), scatter_dimension=1, tiled=True),
    )
    state_weight_sum, conv_state_sum, conv_state_shift_sum, norm_gain_sum = (
        lax.psum_scatter(
            state_weight_grad, ("shard", "ctx", "tp"), scatter_dimension=0, tiled=True
        ),
        lax.psum_scatter(
            conv_weight_grad[:, inner_cols:],
            ("shard", "ctx", "tp"),
            scatter_dimension=1,
            tiled=True,
        ),
        lax.psum_scatter(
            conv_shift_grad[inner_cols:], ("shard", "ctx", "tp"), scatter_dimension=0, tiled=True
        ),
        lax.psum_scatter(norm_gain_grad, ("shard", "ctx", "tp"), scatter_dimension=0, tiled=True),
    )
    head_total = head_sum[0]
    return (
        layer_output,
        input_grad,
        norm_gain_sum,
        gate_weight_sum,
        input_weight_sum,
        step_weight_sum,
        state_weight_sum,
        conv_inner_sum,
        conv_inner_shift_sum,
        conv_state_sum,
        conv_state_shift_sum,
        head_total[:head_count],
        head_total[head_count : 2 * head_count],
        head_total[2 * head_count :],
        gate_gain_sum,
        out_weight_sum,
    )


def solution(mesh):
    return jax.shard_map(
        per_device,
        mesh=mesh,
        in_specs=(
            P(("shard", "ctx", "tp"), None),
            P(("shard", "ctx", "tp"), None),
            P("shard", None),
            P(("shard", "ctx")),
            P(("shard", "ctx"), "tp"),
            P(("shard", "ctx"), "tp"),
            P(("shard", "ctx"), "tp"),
            P(("shard", "ctx"), None),
            P(None, "tp", ("shard", "ctx")),
            P("tp", ("shard", "ctx")),
            P(None, ("shard", "ctx")),
            P(("shard", "ctx")),
            P("tp"),
            P("tp"),
            P("tp"),
            P("tp", ("shard", "ctx")),
            P("tp", ("shard", "ctx")),
        ),
        out_specs=(
            P(("shard", "ctx", "tp"), None),
            P(("shard", "ctx", "tp"), None),
            P(("shard", "ctx", "tp")),
            P(("shard", "ctx"), "tp"),
            P(("shard", "ctx"), "tp"),
            P(("shard", "ctx"), "tp"),
            P(("shard", "ctx", "tp"), None),
            P(None, "tp", ("shard", "ctx")),
            P("tp", ("shard", "ctx")),
            P(None, ("shard", "ctx", "tp")),
            P(("shard", "ctx", "tp")),
            P("tp"),
            P("tp"),
            P("tp"),
            P("tp", ("shard", "ctx")),
            P("tp", ("shard", "ctx")),
        ),
        check_vma=False,
    )
```

profile of v0, /device:TPU:0, one launch (start us, length us, event | category | flops | bytes accessed | tf_op | source)
XLA Modules:
  0.0 1719.6 jit_solution(10445340373977133653)
XLA Ops:
  16.2 69.5 %all-reduce.24 = (bf16[1536]{0:T(1024)(128)(2,1)S(1)}, bf16[256]{0:T(256)(128)(2,1)S(1)}) all-reduce(bf16[1536]{0:T(1024)(128)(2,1)S(1)} %dynamic-update-slice, bf16[256]{0:T(256)(128)(2,1)S(1)} %dynamic-update-slice.1), channel_id=1, replica_groups=mesh['shard'=8,'ctx'=4,'tp'=4] {'shard','ctx'}, use_global_device_ids=true, to_apply=%add.11 | all-reduce | flops 1792 | bytes 7168
  85.7 47.1 %all_gather.66 = bf16[1536,256]{1,0:T(8,128)(2,1)} all-gather(bf16[48,256]{1,0:T(8,128)(2,1)} %param.32), channel_id=1, replica_groups=mesh['shard'=8,'ctx'=4,'tp'=4] {'shard','ctx'}, dimensions={0}, use_global_device_ids=true | all-gather | bytes 811008 | tf_op jit(solution)/shard_map/all_gather | solution.py:210
  135.5 29.5 %all-gather.4 = bf16[32,2,12]{2,1,0:T(2,128)(2,1)S(1)} all-gather(bf16[1,2,12]{2,1,0:T(2,128)(2,1)} %bitcast.669), channel_id=1, replica_groups=mesh['shard'=8,'ctx'=4,'tp'=4] {'shard','ctx'}, dimensions={0}, use_global_device_ids=true | all-gather | bytes 1584 | tf_op jit(solution)/shard_map/all_gather | solution.py:207
  165.9 44.0 %all_gather.67 = bf16[4,12,64]{1,0,2:T(4,128)(2,1)S(1)} all-gather(bf16[4,12,2]{1,0,2:T(4,128)(2,1)S(1)} %copy.249), channel_id=1, replica_groups=mesh['shard'=8,'ctx'=4,'tp'=4] {'shard','ctx'}, dimensions={2}, use_global_device_ids=true | all-gather | bytes 6336 | tf_op jit(solution)/shard_map/all_gather | solution.py:206
  210.1 33.6 %all-gather.5 = bf16[32,8,4]{1,2,0:T(4,128)(2,1)S(1)} all-gather(bf16[1,8,4]{1,2,0:T(4,128)(2,1)} %bitcast.667), channel_id=1, replica_groups=mesh['shard'=8,'ctx'=4,'tp'=4] {'shard','ctx'}, dimensions={0}, use_global_device_ids=true | all-gather | bytes 2112 | tf_op jit(solution)/shard_map/all_gather | solution.py:211
  245.0 34.1 %all-gather.2 = bf16[32,48,12]{1,2,0:T(8,128)(2,1)S(1)} all-gather(bf16[1,48,12]{1,2,0:T(8,128)(2,1)S(1)} %bitcast.662), channel_id=1, replica_groups=mesh['shard'=8,'ctx'=4,'tp'=4] {'shard','ctx'}, dimensions={0}, use_global_device_ids=true | all-gather | bytes 38016 | tf_op jit(solution)/shard_map/all_gather | solution.py:205
  282.5 27.6 %all-gather.6 = bf16[32,2,12]{2,1,0:T(2,128)(2,1)S(1)} all-gather(bf16[1,2,12]{2,1,0:T(2,128)(2,1)S(1)} %bitcast.670), channel_id=1, replica_groups=mesh['shard'=8,'ctx'=4,'tp'=4] {'shard','ctx'}, dimensions={0}, use_global_device_ids=true | all-gather | bytes 1584 | tf_op jit(solution)/shard_map/all_gather | solution.py:208
  334.0 7.3 all-gather.3
  344.9 5.6 multiply_convert_fusion
  358.6 14.3 all-gather
  380.0 202.9 %while.113 = (s32[]{:T(128)}, f32[12,64,128]{2,1,0:T(8,128)S(1)}, s32[]{:T(128)}, f32[4,256,12,64]{1,0,3,2:T(4,128)}, pred[4,256,256,12]{2,1,3,0:T(32,128)(4,1)}...) while((s32[]{:T(128)}, f32[12,64,128]{2,1,0:T(8,128)S(1)}, ...), condition=%wide.region_11.12_spmd.clone, body=%wide.region_8.11_spmd.clone.sunk | while | flops 1318083584 | bytes 27206392 | solution.py:134
  402.2 17.9 %dynamic_update_slice.283 = f32[4,256,12,64]{1,0,3,2:T(4,128)} dynamic-update-slice(f32[4,256,12,64]{1,0,3,2:T(4,128)} %get-tuple-element.2777, f32[1,256,12,64]{1,0,3,2:T(1,128)S(1)} %copy.415, s32[]{:T(128)} %get-tuple-element.2774, s32[]{:T(128)} %constant.260.clone.1..sunk.2, s32[]{:T(128)} %constant.260.clone.1..sunk.2, s32[]{:T(128)} %constant.260.clone.1..sunk.2) | dynamic-update-slice | bytes 1572868 | tf_op jit(solution)/shard_map/jvp()/while/body/jit(dynamic_update_index_in_dim)/dynamic_update_slice | solution.py:134
  453.0 17.9 %dynamic_update_slice.283 = f32[4,256,12,64]{1,0,3,2:T(4,128)} dynamic-update-slice(f32[4,256,12,64]{1,0,3,2:T(4,128)} %get-tuple-element.2777, f32[1,256,12,64]{1,0,3,2:T(1,128)S(1)} %copy.415, s32[]{:T(128)} %get-tuple-element.2774, s32[]{:T(128)} %constant.260.clone.1..sunk.2, s32[]{:T(128)} %constant.260.clone.1..sunk.2, s32[]{:T(128)} %constant.260.clone.1..sunk.2) | dynamic-update-slice | bytes 1572868 | tf_op jit(solution)/shard_map/jvp()/while/body/jit(dynamic_update_index_in_dim)/dynamic_update_slice | solution.py:134
  503.8 17.9 %dynamic_update_slice.283 = f32[4,256,12,64]{1,0,3,2:T(4,128)} dynamic-update-slice(f32[4,256,12,64]{1,0,3,2:T(4,128)} %get-tuple-element.2777, f32[1,256,12,64]{1,0,3,2:T(1,128)S(1)} %copy.415, s32[]{:T(128)} %get-tuple-element.2774, s32[]{:T(128)} %constant.260.clone.1..sunk.2, s32[]{:T(128)} %constant.260.clone.1..sunk.2, s32[]{:T(128)} %constant.260.clone.1..sunk.2) | dynamic-update-slice | bytes 1572868 | tf_op jit(solution)/shard_map/jvp()/while/body/jit(dynamic_update_index_in_dim)/dynamic_update_slice | solution.py:134
  554.5 17.9 %dynamic_update_slice.283 = f32[4,256,12,64]{1,0,3,2:T(4,128)} dynamic-update-slice(f32[4,256,12,64]{1,0,3,2:T(4,128)} %get-tuple-element.2777, f32[1,256,12,64]{1,0,3,2:T(1,128)S(1)} %copy.415, s32[]{:T(128)} %get-tuple-element.2774, s32[]{:T(128)} %constant.260.clone.1..sunk.2, s32[]{:T(128)} %constant.260.clone.1..sunk.2, s32[]{:T(128)} %constant.260.clone.1..sunk.2) | dynamic-update-slice | bytes 1572868 | tf_op jit(solution)/shard_map/jvp()/while/body/jit(dynamic_update_index_in_dim)/dynamic_update_slice | solution.py:134
  589.8 7.9 multiply_reduce_fusion.9
  597.8 23.7 %psum.14 = f32[1024]{0:T(1024)S(1)} all-reduce(f32[1024]{0:T(1024)S(1)} %get-tuple-element.2119), channel_id=1, replica_groups=mesh['shard'=8,'ctx'=4,'tp'=4] {'tp'}, use_global_device_ids=true, to_apply=%region_13.14 | all-reduce | flops 1024 | bytes 8192 | tf_op jit(solution)/shard_map/psum | solution.py:294
  621.6 9.0 multiply_reduce_fusion.5
  630.6 7.7 psum.15
  638.3 8.3 multiply_reduce_fusion.6
  654.8 253.9 %while.114 = (s32[]{:T(128)}, f32[12]{0:T(128)}, f32[12,64,128]{2,1,0:T(8,128)S(1)}, f32[4,256,12,64]{1,0,3,2:T(4,128)}, f32[4,256,128]{2,1,0:T(8,128)}, /*index...) while((s32[]{:T(128)}, f32[12]{0:T(128)}, ...), condition=%wide.region_30.31_spmd.clone, body=%wide.region_18.30_spmd.clone.sunk | while | flops 2628688896 | bytes 34145156 | solution.py:134
  665.0 17.9 %dynamic_update_slice.288 = f32[4,256,12,64]{1,0,3,2:T(4,128)} dynamic-update-slice(f32[4,256,12,64]{1,0,3,2:T(4,128)} %get-tuple-element.2882, f32[1,256,12,64]{1,0,3,2:T(1,128)S(1)} %copy.433, s32[]{:T(128)S(6)} %sub.261, s32[]{:T(128)} %constant.260.clone.1..sunk.3, s32[]{:T(128)} %constant.260.clone.1..sunk.3, s32[]{:T(128)} %constant.260.clone.1..sunk.3) | dynamic-update-slice | bytes 1572868 | tf_op jit(solution)/shard_map/transpose(jvp())/while/body/jit(dynamic_update_index_in_dim)/dynamic_update_slice | solution.py:134
  690.9 7.8 fusion.295
  727.9 17.9 %dynamic_update_slice.288 = f32[4,256,12,64]{1,0,3,2:T(4,128)} dynamic-update-slice(f32[4,256,12,64]{1,0,3,2:T(4,128)} %get-tuple-element.2882, f32[1,256,12,64]{1,0,3,2:T(1,128)S(1)} %copy.433, s32[]{:T(128)S(6)} %sub.261, s32[]{:T(128)} %constant.260.clone.1..sunk.3, s32[]{:T(128)} %constant.260.clone.1..sunk.3, s32[]{:T(128)} %constant.260.clone.1..sunk.3) | dynamic-update-slice | bytes 1572868 | tf_op jit(solution)/shard_map/transpose(jvp())/while/body/jit(dynamic_update_index_in_dim)/dynamic_update_slice | solution.py:134
  753.8 7.8 fusion.295
  791.5 17.9 %dynamic_update_slice.288 = f32[4,256,12,64]{1,0,3,2:T(4,128)} dynamic-update-slice(f32[4,256,12,64]{1,0,3,2:T(4,128)} %get-tuple-element.2882, f32[1,256,12,64]{1,0,3,2:T(1,128)S(1)} %copy.433, s32[]{:T(128)S(6)} %sub.261, s32[]{:T(128)} %constant.260.clone.1..sunk.3, s32[]{:T(128)} %constant.260.clone.1..sunk.3, s32[]{:T(128)} %constant.260.clone.1..sunk.3) | dynamic-update-slice | bytes 1572868 | tf_op jit(solution)/shard_map/transpose(jvp())/while/body/jit(dynamic_update_index_in_dim)/dynamic_update_slice | solution.py:134
  817.4 7.8 fusion.295
  855.0 17.9 %dynamic_update_slice.288 = f32[4,256,12,64]{1,0,3,2:T(4,128)} dynamic-update-slice(f32[4,256,12,64]{1,0,3,2:T(4,128)} %get-tuple-element.2882, f32[1,256,12,64]{1,0,3,2:T(1,128)S(1)} %copy.433, s32[]{:T(128)S(6)} %sub.261, s32[]{:T(128)} %constant.260.clone.1..sunk.3, s32[]{:T(128)} %constant.260.clone.1..sunk.3, s32[]{:T(128)} %constant.260.clone.1..sunk.3) | dynamic-update-slice | bytes 1572868 | tf_op jit(solution)/shard_map/transpose(jvp())/while/body/jit(dynamic_update_index_in_dim)/dynamic_update_slice | solution.py:134
  880.9 7.8 fusion.295
  909.6 9.1 all-gather.7
  926.9 7.6 fusion.210
  943.2 6.5 multiply_reduce_fusion.7
  949.9 9.1 multiply_reduce_fusion.4
  966.6 9.8 pad_add_fusion
  978.3 14.9 reduce-window.71
  1006.5 10.2 add_convert_fusion
  1017.4 7.2 convolution_convert_fusion
  1024.7 7.8 fusion.199
  1032.6 5.8 fusion.211
  1038.8 5.8 fusion.155
  1050.2 342.2 %fusion.2 = f32[16,256]{1,0:T(8,128)S(1)} fusion(f32[1536,256]{1,0:T(8,128)} %fusion.167), kind=kCustom, calls=%all-reduce-scatter | all-reduce-scatter fusion | flops 524289 | bytes 1589248
  1402.1 127.6 %all-reduce.23 = (f32[4,12,64]{1,0,2:T(4,128)S(1)}, f32[12,64]{1,0:T(8,128)S(1)}, f32[32,36]{1,0:T(8,128)S(1)}, f32[12,64]{1,0:T(8,128)S(1)}) all-reduce(f32[4,12,64]{1,0,2:T(4,128)S(1)} %copy.280, f32[12,64]{1,0:T(8,128)S(1)} %reshape.598, ...), channel_id=12, replica_groups=mesh['shard'=8,'ctx'=4,'tp'=4] {'shard','ctx'}, use_global_device_ids=true, to_apply=%region_51.52.clone | all-reduce | flops 5760 | bytes 46080
  1538.6 13.1 collective-permute-start.2
  1568.7 6.2 collective-permute-start.24
  1587.3 5.4 collective-permute-start.3
  1592.7 5.6 collective-permute-start.30
  1619.8 5.6 collective-permute-start.7
  1643.3 64.0 %all-reduce.22 = (f32[1536]{0:T(1024)S(1)}, f32[4,256]{1,0:T(4,128)S(1)}, f32[256]{0:T(256)S(1)}) all-reduce(f32[1536]{0:T(1024)S(1)} %get-tuple-element.1945, f32[4,256]{1,0:T(4,128)S(1)} %pad_add_fusion.4, f32[256]{0:T(256)S(1)} %slice.198), channel_id=7, replica_groups=mesh['shard'=8,'ctx'=4,'tp'=4] {'shard','ctx','tp'}, use_global_device_ids=true, to_apply=%region_42.43.clone | all-reduce | flops 2816 | bytes 22528
  (778 shorter events, 492.8 us)
Async XLA Ops:
  7.2 304.2 %all-gather.15.cloned.1.call-start = ((), (), s32[]{:S(2)}) async-start(), calls=%async_computation.7 | async-start | bytes 3932160 | tf_op jit(solution)/shard_map/all_gather | solution.py:187
  8.0 309.2 %all-gather.17.cloned.1.call-start = ((), (), s32[]{:S(2)}) async-start(), calls=%async_computation.8 | async-start | bytes 2433024 | tf_op jit(solution)/shard_map/all_gather | solution.py:204
  8.7 581.1 %all-gather.19.cloned.1.call-start = ((), (), s32[]{:S(2)}) async-start(), calls=%async_computation.9 | async-start | bytes 2433024 | tf_op jit(solution)/shard_map/all_gather | solution.py:203
  9.4 612.1 %all-gather.21.cloned.1.call-start = ((), (), s32[]{:S(2)}) async-start(), calls=%async_computation.10 | async-start | bytes 2433024 | tf_op jit(solution)/shard_map/all_gather | solution.py:209
  10.0 611.6 %all-gather.23.cloned.1.call-start = ((), (), s32[]{:S(2)}) async-start(), calls=%async_computation.12 | async-start | bytes 3932160 | tf_op jit(solution)/shard_map/all_gather | solution.py:188
  10.6 923.9 %all-gather.25.cloned.1.call-start = ((), (), s32[]{:S(2)}) async-start(), calls=%async_computation.18 | async-start | bytes 1966080 | tf_op jit(solution)/shard_map/all_gather | solution.py:43
  322.8 19.2 %collective-permute-start = (bf16[3,1024]{0,1:T(8,128)(2,1)}, bf16[3,1024]{0,1:T(8,128)(2,1)}, u32[]{:S(2)}, u32[]{:S(2)}) collective-permute-start(bf16[3,1024]{0,1:T(8,128)(2,1)} %slice.218), channel_id=1, source_target_pairs={{0,4},{4,8},{8,12},{1,5},{5,9},{9,13},{2,6},{6,10},{10,14},{3,7},{... | collective-permute-start | bytes 18440 | tf_op jit(solution)/shard_map/ppermute | solution.py:16
  909.5 138.1 %reduce-scatter.19.cloned.1.call-start = ((), (), s32[]{:S(2)}) async-start(), calls=%async_computation.14 | async-start | bytes 655360 | tf_op jit(solution)/shard_map/reduce_scatter | solution.py:358
  976.8 16.6 collective-permute-start.1
  999.1 636.2 %reduce-scatter.27.cloned.1.call-start = ((), (), s32[]{:S(2)}) async-start(), calls=%async_computation.19 | async-start | bytes 811008
  1006.4 634.6 %reduce-scatter.17.cloned.1.call-start = ((), (), s32[]{:S(2)}) async-start(), calls=%async_computation.13 | async-start | bytes 3932160 | tf_op jit(solution)/shard_map/reduce_scatter | solution.py:355
  1016.7 692.4 %reduce-scatter.15.cloned.1.call-start = ((), (), s32[]{:S(2)}) async-start(), calls=%async_computation.11 | async-start | bytes 3932160 | tf_op jit(solution)/shard_map/reduce_scatter | solution.py:300
  1024.7 687.9 %reduce-scatter.25.cloned.1.call-start = ((), (), s32[]{:S(2)}) async-start(), calls=%async_computation.17 | async-start | bytes 4866048 | tf_op jit(solution)/shard_map/reduce_scatter | solution.py:399
  1032.6 680.0 %reduce-scatter.21.cloned.1.call-start = ((), (), s32[]{:S(2)}) async-start(), calls=%async_computation.15 | async-start | bytes 4866048 | tf_op jit(solution)/shard_map/reduce_scatter | solution.py:392
  1038.5 674.1 %reduce-scatter.23.cloned.1.call-start = ((), (), s32[]{:S(2)}) async-start(), calls=%async_computation.16 | async-start | bytes 4866048 | tf_op jit(solution)/shard_map/reduce_scatter | solution.py:393
  1046.7 594.4 %copy-start.41 = (f32[1536]{0:T(1024)S(1)}, f32[1536]{0:T(1024)}, u32[]{:S(2)}) copy-start(f32[1536]{0:T(1024)} %copy-done.40) | copy-start | bytes 18436
  1392.5 8.0 collective-permute-start.10
  1393.9 5.2 collective-permute-start.33
  1395.2 134.5 %collective-permute-start.11 = (f32[16,256]{1,0:T(8,128)S(1)}, f32[16,256]{1,0:T(8,128)S(1)}, u32[]{:S(2)}, u32[]{:S(2)}) collective-permute-start(f32[16,256]{1,0:T(8,128)S(1)} %fusion.2), channel_id=1, source_target_pairs={{0,10},{1,11},{2,12},{3,13},{4,14},{5,15},{6,16},{7,17},{8,18},{9,... | collective-permute-start | bytes 49160
  1396.5 134.5 %collective-permute-start.12 = (f32[16,256]{1,0:T(8,128)S(1)}, f32[16,256]{1,0:T(8,128)S(1)}, u32[]{:S(2)}, u32[]{:S(2)}) collective-permute-start(f32[16,256]{1,0:T(8,128)S(1)} %fusion.2), channel_id=1, source_target_pairs={{0,11},{1,12},{2,13},{3,14},{4,15},{5,16},{6,17},{7,18},{8,19},{9,... | collective-permute-start | bytes 49160
  1397.8 134.6 %collective-permute-start.13 = (f32[16,256]{1,0:T(8,128)S(1)}, f32[16,256]{1,0:T(8,128)S(1)}, u32[]{:S(2)}, u32[]{:S(2)}) collective-permute-start(f32[16,256]{1,0:T(8,128)S(1)} %fusion.2), channel_id=1, source_target_pairs={{0,12},{1,13},{2,14},{3,15},{4,16},{5,17},{6,18},{7,19},{8,20},{9,... | collective-permute-start | bytes 49160
  1399.1 135.9 %collective-permute-start.14 = (f32[16,256]{1,0:T(8,128)S(1)}, f32[16,256]{1,0:T(8,128)S(1)}, u32[]{:S(2)}, u32[]{:S(2)}) collective-permute-start(f32[16,256]{1,0:T(8,128)S(1)} %fusion.2), channel_id=1, source_target_pairs={{0,13},{1,14},{2,15},{3,16},{4,17},{5,18},{6,19},{7,20},{8,21},{9,... | collective-permute-start | bytes 49160
  1400.4 138.2 %collective-permute-start.15 = (f32[16,256]{1,0:T(8,128)S(1)}, f32[16,256]{1,0:T(8,128)S(1)}, u32[]{:S(2)}, u32[]{:S(2)}) collective-permute-start(f32[16,256]{1,0:T(8,128)S(1)} %fusion.2), channel_id=1, source_target_pairs={{0,14},{1,15},{2,16},{3,17},{4,18},{5,19},{6,20},{7,21},{8,22},{9,... | collective-permute-start | bytes 49160
  1529.8 22.6 %collective-permute-start.16 = (f32[16,256]{1,0:T(8,128)S(1)}, f32[16,256]{1,0:T(8,128)S(1)}, u32[]{:S(2)}, u32[]{:S(2)}) collective-permute-start(f32[16,256]{1,0:T(8,128)S(1)} %fusion.2), channel_id=1, source_target_pairs={{0,15},{1,16},{2,17},{3,18},{4,19},{5,20},{6,21},{7,22},{8,23},{9,... | collective-permute-start | bytes 49160
  1531.1 25.3 %collective-permute-start.17 = (f32[16,256]{1,0:T(8,128)S(1)}, f32[16,256]{1,0:T(8,128)S(1)}, u32[]{:S(2)}, u32[]{:S(2)}) collective-permute-start(f32[16,256]{1,0:T(8,128)S(1)} %fusion.2), channel_id=1, source_target_pairs={{0,16},{1,17},{2,18},{3,19},{4,20},{5,21},{6,22},{7,23},{8,24},{9,... | collective-permute-start | bytes 49160
  1532.4 28.5 %collective-permute-start.18 = (f32[16,256]{1,0:T(8,128)S(1)}, f32[16,256]{1,0:T(8,128)S(1)}, u32[]{:S(2)}, u32[]{:S(2)}) collective-permute-start(f32[16,256]{1,0:T(8,128)S(1)} %fusion.2), channel_id=1, source_target_pairs={{0,17},{1,18},{2,19},{3,20},{4,21},{5,22},{6,23},{7,24},{8,25},{9,... | collective-permute-start | bytes 49160
  1535.1 28.7 %collective-permute-start.19 = (f32[16,256]{1,0:T(8,128)S(1)}, f32[16,256]{1,0:T(8,128)S(1)}, u32[]{:S(2)}, u32[]{:S(2)}) collective-permute-start(f32[16,256]{1,0:T(8,128)S(1)} %fusion.2), channel_id=1, source_target_pairs={{0,18},{1,19},{2,20},{3,21},{4,22},{5,23},{6,24},{7,25},{8,26},{9,... | collective-permute-start | bytes 49160
  1538.6 30.0 %collective-permute-start.2 = (f32[16,256]{1,0:T(8,128)S(1)}, f32[16,256]{1,0:T(8,128)S(1)}, u32[]{:S(2)}, u32[]{:S(2)}) collective-permute-start(f32[16,256]{1,0:T(8,128)S(1)} %fusion.2), channel_id=1, source_target_pairs={{0,1},{1,2},{2,3},{3,4},{4,5},{5,6},{6,7},{7,8},{8,9},{9,10},{10,1... | collective-permute-start | bytes 49160
  1552.4 23.1 %collective-permute-start.20 = (f32[16,256]{1,0:T(8,128)S(1)}, f32[16,256]{1,0:T(8,128)S(1)}, u32[]{:S(2)}, u32[]{:S(2)}) collective-permute-start(f32[16,256]{1,0:T(8,128)S(1)} %fusion.2), channel_id=1, source_target_pairs={{0,19},{1,20},{2,21},{3,22},{4,23},{5,24},{6,25},{7,26},{8,27},{9,... | collective-permute-start | bytes 49160
  1556.4 22.5 %collective-permute-start.21 = (f32[16,256]{1,0:T(8,128)S(1)}, f32[16,256]{1,0:T(8,128)S(1)}, u32[]{:S(2)}, u32[]{:S(2)}) collective-permute-start(f32[16,256]{1,0:T(8,128)S(1)} %fusion.2), channel_id=1, source_target_pairs={{0,20},{1,21},{2,22},{3,23},{4,24},{5,25},{6,26},{7,27},{8,28},{9,... | collective-permute-start | bytes 49160
  1560.9 19.8 %collective-permute-start.22 = (f32[16,256]{1,0:T(8,128)S(1)}, f32[16,256]{1,0:T(8,128)S(1)}, u32[]{:S(2)}, u32[]{:S(2)}) collective-permute-start(f32[16,256]{1,0:T(8,128)S(1)} %fusion.2), channel_id=1, source_target_pairs={{0,21},{1,22},{2,23},{3,24},{4,25},{5,26},{6,27},{7,28},{8,29},{9,... | collective-permute-start | bytes 49160
  1563.8 20.3 %collective-permute-start.23 = (f32[16,256]{1,0:T(8,128)S(1)}, f32[16,256]{1,0:T(8,128)S(1)}, u32[]{:S(2)}, u32[]{:S(2)}) collective-permute-start(f32[16,256]{1,0:T(8,128)S(1)} %fusion.2), channel_id=1, source_target_pairs={{0,22},{1,23},{2,24},{3,25},{4,26},{5,27},{6,28},{7,29},{8,30},{9,... | collective-permute-start | bytes 49160
  1568.7 16.9 collective-permute-start.24
  1575.5 11.8 collective-permute-start.25
  1578.9 13.8 collective-permute-start.26
  1580.7 17.6 %collective-permute-start.27 = (f32[16,256]{1,0:T(8,128)S(1)}, f32[16,256]{1,0:T(8,128)S(1)}, u32[]{:S(2)}, u32[]{:S(2)}) collective-permute-start(f32[16,256]{1,0:T(8,128)S(1)} %fusion.2), channel_id=1, source_target_pairs={{0,26},{1,27},{2,28},{3,29},{4,30},{5,31},{6,32},{7,33},{8,34},{9,... | collective-permute-start | bytes 49160
  1584.1 19.6 %collective-permute-start.28 = (f32[16,256]{1,0:T(8,128)S(1)}, f32[16,256]{1,0:T(8,128)S(1)}, u32[]{:S(2)}, u32[]{:S(2)}) collective-permute-start(f32[16,256]{1,0:T(8,128)S(1)} %fusion.2), channel_id=1, source_target_pairs={{0,27},{1,28},{2,29},{3,30},{4,31},{5,32},{6,33},{7,34},{8,35},{9,... | collective-permute-start | bytes 49160
  1585.6 22.1 %collective-permute-start.29 = (f32[16,256]{1,0:T(8,128)S(1)}, f32[16,256]{1,0:T(8,128)S(1)}, u32[]{:S(2)}, u32[]{:S(2)}) collective-permute-start(f32[16,256]{1,0:T(8,128)S(1)} %fusion.2), channel_id=1, source_target_pairs={{0,28},{1,29},{2,30},{3,31},{4,32},{5,33},{6,34},{7,35},{8,36},{9,... | collective-permute-start | bytes 49160
  1587.3 24.8 %collective-permute-start.3 = (f32[16,256]{1,0:T(8,128)S(1)}, f32[16,256]{1,0:T(8,128)S(1)}, u32[]{:S(2)}, u32[]{:S(2)}) collective-permute-start(f32[16,256]{1,0:T(8,128)S(1)} %fusion.2), channel_id=1, source_target_pairs={{0,2},{1,3},{2,4},{3,5},{4,6},{5,7},{6,8},{7,9},{8,10},{9,11},{10,... | collective-permute-start | bytes 49160
  1592.7 22.5 %collective-permute-start.30 = (f32[16,256]{1,0:T(8,128)S(1)}, f32[16,256]{1,0:T(8,128)S(1)}, u32[]{:S(2)}, u32[]{:S(2)}) collective-permute-start(f32[16,256]{1,0:T(8,128)S(1)} %fusion.2), channel_id=1, source_target_pairs={{0,29},{1,30},{2,31},{3,32},{4,33},{5,34},{6,35},{7,36},{8,37},{9,... | collective-permute-start | bytes 49160
  1598.3 21.5 %collective-permute-start.31 = (f32[16,256]{1,0:T(8,128)S(1)}, f32[16,256]{1,0:T(8,128)S(1)}, u32[]{:S(2)}, u32[]{:S(2)}) collective-permute-start(f32[16,256]{1,0:T(8,128)S(1)} %fusion.2), channel_id=1, source_target_pairs={{0,30},{1,31},{2,32},{3,33},{4,34},{5,35},{6,36},{7,37},{8,38},{9,... | collective-permute-start | bytes 49160
  1603.7 21.7 %collective-permute-start.32 = (f32[16,256]{1,0:T(8,128)S(1)}, f32[16,256]{1,0:T(8,128)S(1)}, u32[]{:S(2)}, u32[]{:S(2)}) collective-permute-start(f32[16,256]{1,0:T(8,128)S(1)} %fusion.2), channel_id=1, source_target_pairs={{0,31},{1,32},{2,33},{3,34},{4,35},{5,36},{6,37},{7,38},{8,39},{9,... | collective-permute-start | bytes 49160
  1607.7 20.9 %collective-permute-start.4 = (f32[16,256]{1,0:T(8,128)S(1)}, f32[16,256]{1,0:T(8,128)S(1)}, u32[]{:S(2)}, u32[]{:S(2)}) collective-permute-start(f32[16,256]{1,0:T(8,128)S(1)} %fusion.2), channel_id=1, source_target_pairs={{0,3},{1,4},{2,5},{3,6},{4,7},{5,8},{6,9},{7,10},{8,11},{9,12},{10... | collective-permute-start | bytes 49160
  1612.0 24.7 %collective-permute-start.5 = (f32[16,256]{1,0:T(8,128)S(1)}, f32[16,256]{1,0:T(8,128)S(1)}, u32[]{:S(2)}, u32[]{:S(2)}) collective-permute-start(f32[16,256]{1,0:T(8,128)S(1)} %fusion.2), channel_id=1, source_target_pairs={{0,4},{1,5},{2,6},{3,7},{4,8},{5,9},{6,10},{7,11},{8,12},{9,13},{1... | collective-permute-start | bytes 49160
  1615.2 21.6 %collective-permute-start.6 = (f32[16,256]{1,0:T(8,128)S(1)}, f32[16,256]{1,0:T(8,128)S(1)}, u32[]{:S(2)}, u32[]{:S(2)}) collective-permute-start(f32[16,256]{1,0:T(8,128)S(1)} %fusion.2), channel_id=1, source_target_pairs={{0,5},{1,6},{2,7},{3,8},{4,9},{5,10},{6,11},{7,12},{8,13},{9,14},{... | collective-permute-start | bytes 49160
  1619.8 17.0 collective-permute-start.7
  1625.4 11.3 collective-permute-start.8
  1628.6 8.2 collective-permute-start.9
  (92 other events, 4331.1 us)
Sparse Core Ops, SparseCore 0:
  9.7 42.0 all-gather.14
  54.1 44.5 all-gather.16
  101.0 43.4 all-gather.18
  146.7 43.5 all-gather.20
  191.8 38.8 all-gather.22
  909.7 23.6 all-gather.24
  999.2 20.9 reduce-scatter.18
  1024.3 77.3 reduce-scatter.26
  1104.0 39.4 reduce-scatter.16
  1145.8 40.2 reduce-scatter.14
  1190.4 83.4 reduce-scatter.24
  1278.5 82.9 reduce-scatter.20
  1365.7 83.5 reduce-scatter.22
where the time goes:
time: 1740 us; the launch traced here: 1720 us
  blocking collectives  881 us (51%)
  local copies, waits for them, and re-layouts  293 us (17%)
  matrix products  219 us (13%)
  other arithmetic  183 us (11%)
  starting transfers between devices  117 us (7%)
  between operations  19.4 us (1%)
    unnamed x4, blocking collectives  603 us
    dynamic_update_slice x48, local copies, waits for them, and re-layouts, device_outputs(): lax.scan(step_fn, (state_start, seg_before), (inner_x.reshape(blocks, STR...  173 us
    unnamed x33, starting transfers between devices  111 us
    dot_general x12, matrix products, block_step(): local_out = jnp.einsum('tsh,shp->thp', scores, inner_x, precision=HIGH)  67 us
    all_gather x1, blocking collectives, per_device(): lax.all_gather(proj_state, ('shard', 'ctx'), axis=0, tiled=True)  47.1 us
    dynamic_update_slice x24, other arithmetic, device_outputs(): lax.scan(step_fn, (state_start, seg_before), (inner_x.reshape(blocks, STR...  44.5 us
    all_gather x1, blocking collectives, per_device(): lax.all_gather(conv_inner, ('shard', 'ctx'), axis=2, tiled=True)  44 us
    another operation x51, other arithmetic  36.4 us
  transfers between devices with their start and end apart: 47, of which 0 were waited for; matrix products, arithmetic and copies ran while one was open for 41% of the time, Pallas kernels for 0%

commit v1 on v0

v1 whole, which is shorter than its diff:
```python
import functools

import jax
import jax.numpy as jnp
from jax import lax
from jax.experimental import pallas as pl
from jax.experimental.pallas import tpu as pltpu
from jax.sharding import PartitionSpec as P

MESH = pl.DeviceIdType.MESH
ANY = pl.ANY
F32 = jnp.float32
BF16 = jnp.bfloat16
EPS = 1e-05
LOG2E = 1.4426950408889634
HIGH = lax.Precision.HIGHEST

D = 1536
ROWS = 1024
HD = 768
HEADS = 12
PAIRS = 6
NS = 128
CONV = 1024
LEN = 128
CHUNKS = 8
E_ALL = 3072
C_OUT, C_GATE, C_IN, C_BC, C_MISC, WIDE = 0, 768, 1536, 2304, 2560, 2688
HALF_A, HALF_A1, HALF_B1 = 1408, 768, 2048


def dot(a, b):
    return jnp.dot(a, b, preferred_element_type=F32)


def dot_nt(a, b):
    return lax.dot_general(a, b, (((1,), (1,)), ((), ())), preferred_element_type=F32)


def dot_tn(a, b):
    return lax.dot_general(a, b, (((0,), (0,)), ((), ())), preferred_element_type=F32)


def dot_full(a, b):
    return jnp.dot(a, b, precision=HIGH, preferred_element_type=F32)


def iota(shape, axis):
    return lax.broadcasted_iota(jnp.int32, shape, axis)


def place():
    s = lax.axis_index("shard")
    return s // 2, s % 2, lax.axis_index("ctx"), lax.axis_index("tp")


def device(x, c, z, y):
    return {"shard": x * 2 + c, "ctx": z, "tp": y}


def enter(others):
    barrier = pltpu.get_barrier_semaphore()
    for other in others:
        pl.semaphore_signal(barrier, inc=1, device_id=other, device_id_type=MESH)
    pl.semaphore_wait(barrier, len(others))


class Sends:
    def __init__(self, send_sem, recv_sem):
        self.send_sem, self.recv_sem, self.copies = send_sem, recv_sem, []

    def __call__(self, src, dst, to):
        k = len(self.copies)
        copy = pltpu.make_async_remote_copy(
            src_ref=src,
            dst_ref=dst,
            send_sem=self.send_sem.at[k],
            recv_sem=self.recv_sem.at[k],
            device_id=to,
            device_id_type=MESH,
        )
        copy.start()
        self.copies.append(copy)
        return copy

    def finish(self):
        for copy in self.copies:
            copy.wait_send()


def sems(n):
    return [pltpu.SemaphoreType.DMA((n,)), pltpu.SemaphoreType.DMA((n,)), pltpu.SemaphoreType.DMA((4,))]


def comm_params(collective_id, vmem=None):
    return pltpu.CompilerParams(
        collective_id=collective_id, has_side_effects=True, vmem_limit_bytes=vmem
    )


def shape(dims, kind):
    return jax.ShapeDtypeStruct(dims, kind)


def gather_kernel(w_ref, x_ref, W, X, E, ssem, rsem, lsem):
    x, c, z, y = place()
    xr, xl, xo = (x + 1) % 4, (x + 3) % 4, (x + 2) % 4
    zr, zl, zo = (z + 1) % 4, (z + 3) % 4, (z + 2) % 4
    yr, yl = (y + 1) % 4, (y + 3) % 4
    dxr, dxl = device(xr, c, z, y), device(xl, c, z, y)
    dzr, dzl = device(x, c, zr, y), device(x, c, zl, y)
    dyr, dyl = device(x, c, z, yr), device(x, c, z, yl)
    dco = device(x, 1 - c, z, y)
    enter([dxr, dxl, dzr, dzl, dyr, dyl, dco])
    go = Sends(ssem, rsem)
    A, A1, A2 = pl.ds(0, HALF_A), pl.ds(0, HALF_A1), pl.ds(HALF_A1, HALF_A - HALF_A1)
    B = pl.ds(HALF_A, WIDE - HALF_A)
    B1, B2 = pl.ds(HALF_A, HALF_B1 - HALF_A), pl.ds(HALF_B1, WIDE - HALF_B1)
    H1, H2 = pl.ds(0, 128), pl.ds(128, 128)

    a_r = go(w_ref.at[:, A], W.at[x, c, z, :, A], dzr)
    b_r = go(w_ref.at[:, B], W.at[x, c, z, :, B], dxr)
    a_l = go(w_ref.at[:, A], W.at[x, c, z, :, A], dzl)
    b_l = go(w_ref.at[:, B], W.at[x, c, z, :, B], dxl)
    x_r = go(x_ref, X.at[y], dyr)
    x_l = go(x_ref, X.at[y], dyl)
    own = pltpu.make_async_copy(w_ref, W.at[x, c, z], lsem.at[0])
    own.start()
    own_x = pltpu.make_async_copy(x_ref, X.at[y], lsem.at[1])
    own_x.start()

    def on_x(xx, cols):
        return W.at[xx, c, :, :, cols]

    def on_z(zz, cols):
        return W.at[:, c, zz, :, cols]

    def same(ref, to):
        return go(ref, ref, to)

    a_r.wait_recv()
    a_fr = same(W.at[x, c, zl, :, A1], dzr)
    b_r.wait_recv()
    b_fr = same(W.at[xl, c, z, :, B1], dxr)
    a_l.wait_recv()
    a_fl = same(W.at[x, c, zr, :, A2], dzl)
    b_l.wait_recv()
    b_fl = same(W.at[xr, c, z, :, B2], dxl)
    own.wait()
    a_fr.wait_recv()
    a_fl.wait_recv()
    a2_r = same(on_x(x, A), dxr)
    a2_l = same(on_x(x, A), dxl)
    b_fr.wait_recv()
    b_fl.wait_recv()
    b2_r = same(on_z(z, B), dzr)
    b2_l = same(on_z(z, B), dzl)
    last = [same(on_x(x, A), dco), same(on_z(z, B), dco)]
    x_r.wait_recv()
    x_fr = same(X.at[yl, H1], dyr)
    x_l.wait_recv()
    x_fl = same(X.at[yr, H2], dyl)
    a2_r.wait_recv()
    f1 = same(on_x(xl, A1), dxr)
    last.append(same(on_x(xl, A), dco))
    b2_r.wait_recv()
    f3 = same(on_z(zl, B1), dzr)
    last.append(same(on_z(zl, B), dco))
    a2_l.wait_recv()
    f2 = same(on_x(xr, A2), dxl)
    last.append(same(on_x(xr, A), dco))
    b2_l.wait_recv()
    f4 = same(on_z(zr, B2), dzl)
    last.append(same(on_z(zr, B), dco))
    own_x.wait()
    x_fr.wait_recv()
    x_fl.wait_recv()
    edge = go(X.at[3, pl.ds(240, 16)], E, dzr)
    f1.wait_recv()
    last.append(same(on_x(xo, A1), dco))
    f3.wait_recv()
    last.append(same(on_z(zo, B1), dco))
    f2.wait_recv()
    last.append(same(on_x(xo, A2), dco))
    f4.wait_recv()
    last.append(same(on_z(zo, B2), dco))
    edge.wait_recv()
    for copy in last:
        copy.wait_recv()
    go.finish()


def gather(pack, rows):
    return pl.pallas_call(
        gather_kernel,
        out_shape=(
            shape((4, 2, 4, 48, WIDE), BF16),
            shape((4, 256, D), BF16),
            shape((16, D), BF16),
        ),
        in_specs=[pl.BlockSpec(memory_space=ANY)] * 2,
        out_specs=[pl.BlockSpec(memory_space=ANY)] * 3,
        scratch_shapes=sems(40),
        compiler_params=comm_params(0),
        name="gather_weights",
    )(pack, rows)


def swap_kernel(axis, own_ref, out_ref, ssem, rsem, lsem):
    x, c, z, y = place()

    def along(k):
        if axis == "ctx":
            return device(x, c, (z + k) % 4, y)
        return device(x, c, z, (y + k) % 4)

    me = z if axis == "ctx" else y
    others = [along(k) for k in (1, 3, 2)]
    enter(others)
    go = Sends(ssem, rsem)
    for other in others:
        go(own_ref, out_ref.at[me], other)
    own = pltpu.make_async_copy(own_ref, out_ref.at[me], lsem.at[0])
    own.start()
    own.wait()
    for copy in go.copies:
        copy.wait_recv()
    go.finish()


def swap(a, axis, collective_id, name):
    return pl.pallas_call(
        functools.partial(swap_kernel, axis),
        out_shape=shape((4,) + a.shape, a.dtype),
        in_specs=[pl.BlockSpec(memory_space=ANY)],
        out_specs=pl.BlockSpec(memory_space=ANY),
        scratch_shapes=sems(4),
        compiler_params=comm_params(collective_id),
        name=name,
    )(a)


def edge_kernel(own_ref, out_ref, ssem, rsem, lsem):
    x, c, z, y = place()
    before, after = device(x, c, (z + 3) % 4, y), device(x, c, (z + 1) % 4, y)
    enter([before, after])
    go = Sends(ssem, rsem)
    copy = go(own_ref, out_ref, before)
    copy.wait_recv()
    go.finish()


def edge_back(a, collective_id):
    return pl.pallas_call(
        edge_kernel,
        out_shape=shape(a.shape, a.dtype),
        in_specs=[pl.BlockSpec(memory_space=ANY)],
        out_specs=pl.BlockSpec(memory_space=ANY),
        scratch_shapes=sems(2),
        compiler_params=comm_params(collective_id),
        name="edge_back",
    )(a)


def spread_heads(v, p):
    r = v.shape[0]
    low = jnp.broadcast_to(v[:, 2 * p : 2 * p + 1], (r, 128))
    high = jnp.broadcast_to(v[:, 2 * p + 1 : 2 * p + 2], (r, 128))
    return jnp.where(iota((r, 128), 1) < 64, low, high)


def cols(p):
    return slice(128 * p, 128 * p + 128)


def stacked(pair):
    lane = iota(pair.shape, 1)
    zero = jnp.zeros_like(pair)
    return jnp.concatenate([jnp.where(lane < 64, pair, zero), jnp.where(lane < 64, zero, pair)], axis=0)


def in_two(v):
    high = v.astype(BF16)
    return high, (v - high.astype(F32)).astype(BF16)


def twice(v):
    return jnp.concatenate([v, v], axis=1)


def link_rows(decay):
    high, low = in_two(jnp.broadcast_to(decay, (8, HD)))
    return jnp.concatenate([high, low], axis=0)


def link_of(summ_ref, j):
    both = summ_ref[j, NS : NS + 16, :].astype(F32)
    return both[0:1] + both[8:9]


def head_sum(pair, p):
    lane, head = iota((128, 128), 0), iota((128, 128), 1)
    pick = jnp.where(head == 2 * p + lane // 64, 1.0, 0.0).astype(BF16)
    return dot(pair.astype(BF16), pick)


def triangle(kind):
    t, s = iota((LEN, LEN), 0), iota((LEN, LEN), 1)
    keep = {"incl": s <= t, "suffix": s >= t, "strict": s < t}[kind]
    return jnp.where(keep, 1.0, 0.0).astype(F32)


def fold8(v):
    return jnp.sum(v.reshape(v.shape[0] // 8, 8, v.shape[1]), axis=0)


def front_kernel(
    x_ref, w_ref, e_ref, gain_ref, conv_ref, step_ref, pos_ref,
    normed_ref, gate_ref, ci_ref, edge_ref, ds_ref, xbc_ref, xdt_ref, dt_ref, cum_ref, sig_ref, fresh_ref, summ_ref,
    buf, state, decay,
):
    step = pl.program_id(0)
    tile = x_ref.shape[0]

    def norm(rows):
        wide = rows.astype(F32)
        r = lax.rsqrt(jnp.mean(wide * wide, axis=1, keepdims=True) + EPS)
        return (wide * r * gain_ref[...]).astype(BF16)

    @pl.when(step == 0)
    def _():
        edge = dot(norm(e_ref[...]), w_ref[:, C_IN:C_MISC]).astype(BF16)
        edge_ref[...] = edge
        buf[0:8, :] = edge.astype(F32)[8:16]
        state[...] = jnp.zeros_like(state)
        decay[...] = jnp.ones_like(decay)

    @pl.when(step > 0)
    def _():
        buf[0:8, :] = buf[tile : tile + 8, :]

    normed = norm(x_ref[...])
    normed_ref[...] = normed
    gate_ref[...] = dot(normed, w_ref[:, C_GATE:C_IN])
    conv_in = dot(normed, w_ref[:, C_IN:C_MISC]).astype(BF16)
    ci_ref[...] = conv_in
    buf[8 : 8 + tile, :] = conv_in.astype(F32)
    step_pre = dot(normed, w_ref[:, C_MISC:WIDE])

    pos = pos_ref[...]
    for j in range(CONV // 128):
        lanes = cols(j)
        acc = buf[8 : 8 + tile, lanes] * conv_ref[3:4, lanes] + conv_ref[4:5, lanes]
        for back in (1, 2, 3):
            term = buf[8 - back : 8 - back + tile, lanes] * conv_ref[3 - back : 4 - back, lanes]
            acc = acc + jnp.where(pos >= back, term, 0.0)
        sig = jax.nn.sigmoid(acc)
        ds_ref[:, lanes] = sig * (1.0 + acc * (1.0 - sig))
        xbc_ref[:, lanes] = (acc * sig).astype(BF16)

    lane = iota((tile, 128), 1)
    pre = step_pre + step_ref[0:1, :]
    small = jnp.exp(-jnp.abs(pre))
    log1p = jnp.where(small < 1e-3, small * (1.0 - 0.5 * small + (1.0 / 3.0) * small * small), jnp.log(1.0 + small))
    dt = jnp.where(lane < HEADS, jnp.maximum(pre, 0.0) + log1p, 0.0)
    dt_ref[...] = dt
    sig_ref[...] = jax.nn.sigmoid(pre)
    rate = dt * step_ref[1:2, :]
    for sub in range(tile // LEN):
        rows = slice(LEN * sub, LEN * sub + LEN)
        cum = dot_full(triangle("incl"), rate[rows])
        cum_ref[rows, :] = cum
        last = cum[LEN - 1 : LEN, :]
        pos_last = pos[LEN * sub + LEN - 1 : LEN * sub + LEN, :]
        row = iota((LEN, 128), 0).astype(F32)
        fade = jnp.where((LEN - 1) - row <= pos_last, jnp.exp2(last - cum), 0.0)
        whole = jnp.where(pos_last > LEN - 1, jnp.exp2(last), 0.0)
        basis_t = jnp.transpose(xbc_ref[rows, HD : HD + NS].astype(F32)).astype(BF16)
        for p in range(PAIRS):
            xdt = (xbc_ref[rows, cols(p)].astype(F32) * spread_heads(dt[rows], p)).astype(BF16)
            xdt_ref[rows, cols(p)] = xdt
            ended = (xdt.astype(F32) * spread_heads(fade, p)).astype(BF16)
            fresh = dot(basis_t, ended)
            fresh_ref[sub, :, cols(p)] = fresh
            factor = spread_heads(whole, p)
            state[:, cols(p)] = state[:, cols(p)] * factor + fresh
            decay[:, cols(p)] = decay[:, cols(p)] * factor

    @pl.when(step == pl.num_programs(0) - 1)
    def _():
        summ_ref[0:NS, :] = state[...].astype(BF16)
        summ_ref[NS : NS + 16, :] = link_rows(decay[...])


def whole_spec(*dims):
    return pl.BlockSpec(dims, lambda i: (0,) * len(dims), pipeline_mode=pl.Buffered(1))


def rows_spec(r, c, back=None):
    if back is None:
        return pl.BlockSpec((r, c), lambda i: (i, 0))
    return pl.BlockSpec((r, c), lambda i: (back - i, 0))


def front(X, W, E, gain, conv, step, pos):
    tile = 256
    sub = tile // LEN
    return pl.pallas_call(
        front_kernel,
        grid=(ROWS // tile,),
        in_specs=[
            rows_spec(tile, D), whole_spec(D, WIDE), whole_spec(16, D), whole_spec(1, D), whole_spec(8, CONV),
            whole_spec(8, 128), rows_spec(tile, 128),
        ],
        out_specs=[
            rows_spec(tile, D), rows_spec(tile, HD), rows_spec(tile, CONV), whole_spec(16, CONV), rows_spec(tile, CONV),
            rows_spec(tile, CONV), rows_spec(tile, HD), rows_spec(tile, 128), rows_spec(tile, 128), rows_spec(tile, 128),
            pl.BlockSpec((sub, NS, HD), lambda i: (i, 0, 0)), whole_spec(NS + 16, HD),
        ],
        out_shape=[
            shape((ROWS, D), BF16), shape((ROWS, HD), F32), shape((ROWS, CONV), BF16), shape((16, CONV), BF16),
            shape((ROWS, CONV), F32), shape((ROWS, CONV), BF16), shape((ROWS, HD), BF16), shape((ROWS, 128), F32),
            shape((ROWS, 128), F32), shape((ROWS, 128), F32), shape((CHUNKS, NS, HD), F32), shape((NS + 16, HD), BF16),
        ],
        scratch_shapes=[pltpu.VMEM((8 + tile, CONV), F32), pltpu.VMEM((NS, HD), F32), pltpu.VMEM((1, HD), F32)],
        compiler_params=pltpu.CompilerParams(vmem_limit_bytes=56 << 20),
        cost_estimate=pl.CostEstimate(flops=2 * ROWS * D * 1920, bytes_accessed=40 << 20, transcendentals=ROWS * CONV),
        name="front",
    )(X, W, E, gain, conv, step, pos)


def scan_kernel(
    xbc_ref, xdt_ref, cum_ref, fresh_ref, gate_ref, pos_ref, summ_ref, cot_ref, w_ref, skip_ref, gain_ref,
    mixed_ref, db_ref, sums_ref, enter_ref,
    state,
):
    step = pl.program_id(0)
    tile = xbc_ref.shape[0]

    @pl.when(step == 0)
    def _():
        z = lax.axis_index("ctx")
        start = jnp.zeros((NS, HD), F32)
        for j in range(3):
            link = link_of(summ_ref, j)
            start = jnp.where(j < z, start * link + summ_ref[j, 0:NS, :].astype(F32), start)
        state[...] = start

    db_ref[...] = dot(cot_ref[...], w_ref[...])
    t, s = iota((LEN, LEN), 0), iota((LEN, LEN), 1)
    gap = (t - s).astype(F32)
    for sub in range(tile // LEN):
        rows = slice(LEN * sub, LEN * sub + LEN)
        pos = pos_ref[rows, :]
        keep = (gap >= 0) & (gap <= pos)
        cum = cum_ref[rows, :]
        cum_t = jnp.transpose(cum)
        basis = xbc_ref[rows, HD : HD + NS]
        basis_c = xbc_ref[rows, HD + NS : CONV]
        inner = dot_nt(basis_c, basis)
        fade = jnp.where(pos > t.astype(F32), jnp.exp2(cum), 0.0)
        whole = jnp.where(pos[LEN - 1 : LEN] > LEN - 1, jnp.exp2(cum[LEN - 1 : LEN]), 0.0)
        square = jnp.zeros((LEN, 128), F32)
        cross = jnp.zeros((LEN, 128), F32)
        for p in range(PAIRS):
            lanes = cols(p)
            entered = state[:, lanes].astype(BF16)
            enter_ref[sub, :, lanes] = entered
            parts = []
            for h in (2 * p, 2 * p + 1):
                span = jnp.where(keep, cum[:, h : h + 1] - cum_t[h : h + 1, :], -1e30)
                parts.append((jnp.exp2(span) * inner).astype(BF16))
            local = dot(jnp.concatenate(parts, axis=1), stacked(xdt_ref[rows, lanes]))
            out = local + dot(basis_c, entered) * spread_heads(fade, p)
            mixed = out + skip_ref[:, lanes] * xbc_ref[rows, lanes].astype(F32)
            mixed_ref[rows, lanes] = mixed
            gate = gate_ref[rows, lanes]
            gated = mixed * gate * jax.nn.sigmoid(gate)
            square = square + gated * gated
            cross = cross + gated * gain_ref[:, lanes] * db_ref[rows, lanes]
            state[:, lanes] = state[:, lanes] * spread_heads(whole, p) + fresh_ref[sub, :, lanes]
        sq = jnp.sum(square, axis=1, keepdims=True)
        cr = jnp.sum(cross, axis=1, keepdims=True)
        both = jnp.where(s == 0, sq, jnp.where(s == 1, cr, 0.0))
        sums_ref[8 * sub : 8 * sub + 8, :] = jnp.transpose(both)[0:8]


def scan(xbc, xdt, cum, fresh, gate, pos, summs, cot, W, skip, gain):
    tile = 256
    sub = tile // LEN
    return pl.pallas_call(
        scan_kernel,
        grid=(ROWS // tile,),
        in_specs=[
            rows_spec(tile, CONV), rows_spec(tile, HD), rows_spec(tile, 128),
            pl.BlockSpec((sub, NS, HD), lambda i: (i, 0, 0)), rows_spec(tile, HD), rows_spec(tile, 128),
            whole_spec(4, NS + 16, HD), rows_spec(tile, D), whole_spec(D, HD), whole_spec(1, HD), whole_spec(1, HD),
        ],
        out_specs=[
            rows_spec(tile, HD), rows_spec(tile, HD), rows_spec(8 * sub, 128),
            pl.BlockSpec((sub, NS, HD), lambda i: (i, 0, 0)),
        ],
        out_shape=[
            shape((ROWS, HD), F32), shape((ROWS, HD), F32), shape((8 * CHUNKS, 128), F32), shape((CHUNKS, NS, HD), BF16),
        ],
        scratch_shapes=[pltpu.VMEM((NS, HD), F32)],
        compiler_params=pltpu.CompilerParams(vmem_limit_bytes=56 << 20),
        cost_estimate=pl.CostEstimate(flops=2 * ROWS * D * 900, bytes_accessed=30 << 20, transcendentals=ROWS * CONV),
        name="scan",
    )(xbc, xdt, cum, fresh, gate, pos, summs, cot, W, skip, gain)


def turn_kernel(
    sums_ref, mixed_ref, gate_ref, db_ref, xbc_ref, cum_ref, pos_ref, w_ref, gain_ref,
    branch_ref, dgate_ref, dmix_ref, out_ref, gfresh_ref, summ_ref, acc_ref,
    state, decay,
):
    step = pl.program_id(0)
    tile = mixed_ref.shape[0]

    @pl.when(step == 0)
    def _():
        state[...] = jnp.zeros_like(state)
        decay[...] = jnp.ones_like(decay)
        acc_ref[...] = jnp.zeros_like(acc_ref)

    for sub in reversed(range(tile // LEN)):
        rows = slice(LEN * sub, LEN * sub + LEN)
        total = sums_ref[0, 8 * sub : 8 * sub + 8, :]
        for k in range(1, 4):
            total = total + sums_ref[k, 8 * sub : 8 * sub + 8, :]
        both = jnp.transpose(jnp.concatenate([total, jnp.zeros((120, 128), F32)], axis=0))
        r = lax.rsqrt(both[:, 0:1] * (1.0 / E_ALL) + EPS)
        slope = r * r * r * both[:, 1:2] * (1.0 / E_ALL)
        pos = pos_ref[rows, :]
        cum = cum_ref[rows, :]
        fade = jnp.where(pos > iota((LEN, 128), 0).astype(F32), jnp.exp2(cum), 0.0)
        whole = jnp.where(pos[LEN - 1 : LEN] > LEN - 1, jnp.exp2(cum[LEN - 1 : LEN]), 0.0)
        basis_t = jnp.transpose(xbc_ref[rows, HD + NS : CONV].astype(F32)).astype(BF16)
        for p in range(PAIRS):
            lanes = cols(p)
            mixed, gate, db = mixed_ref[rows, lanes], gate_ref[rows, lanes], db_ref[rows, lanes]
            gain = gain_ref[:, lanes]
            sig = jax.nn.sigmoid(gate)
            silu = gate * sig
            gated = mixed * silu
            scaled = gated * r
            branch_ref[rows, lanes] = (scaled * gain).astype(BF16)
            acc_ref[0:8, lanes] += fold8(db * scaled)
            dgated = r * gain * db - gated * slope
            dmix = dgated * silu
            dgate_ref[rows, lanes] = (dgated * mixed * sig * (1.0 + gate * (1.0 - sig))).astype(BF16)
            dmix_ref[rows, lanes] = dmix
            acc_ref[8:16, lanes] += fold8(dmix * xbc_ref[rows, lanes].astype(F32))
            fresh = dot(basis_t, (dmix * spread_heads(fade, p)).astype(BF16))
            gfresh_ref[sub, :, lanes] = fresh
            factor = spread_heads(whole, p)
            state[:, lanes] = state[:, lanes] * factor + fresh
            decay[:, lanes] = decay[:, lanes] * factor
    out_ref[...] = dot_nt(branch_ref[...], w_ref[...]).astype(BF16)

    @pl.when(step == pl.num_programs(0) - 1)
    def _():
        summ_ref[0:NS, :] = state[...].astype(BF16)
        summ_ref[NS : NS + 16, :] = link_rows(decay[...])


def turn(sums, mixed, gate, db, xbc, cum, pos, W, gain):
    tile = 256
    sub = tile // LEN
    top = ROWS // tile - 1
    return pl.pallas_call(
        turn_kernel,
        grid=(ROWS // tile,),
        in_specs=[
            pl.BlockSpec((4, 8 * sub, 128), lambda i: (0, top - i, 0)), rows_spec(tile, HD, top), rows_spec(tile, HD, top),
            rows_spec(tile, HD, top), rows_spec(tile, CONV, top), rows_spec(tile, 128, top), rows_spec(tile, 128, top),
            whole_spec(D, HD), whole_spec(1, HD),
        ],
        out_specs=[
            rows_spec(tile, HD, top), rows_spec(tile, HD, top), rows_spec(tile, HD, top), rows_spec(tile, D, top),
            pl.BlockSpec((sub, NS, HD), lambda i: (top - i, 0, 0)), whole_spec(NS + 16, HD), whole_spec(16, HD),
        ],
        out_shape=[
            shape((ROWS, HD), BF16), shape((ROWS, HD), BF16), shape((ROWS, HD), F32), shape((ROWS, D), BF16),
            shape((CHUNKS, NS, HD), F32), shape((NS + 16, HD), BF16), shape((16, HD), F32),
        ],
        scratch_shapes=[pltpu.VMEM((NS, HD), F32), pltpu.VMEM((1, HD), F32)],
        compiler_params=pltpu.CompilerParams(vmem_limit_bytes=56 << 20),
        cost_estimate=pl.CostEstimate(flops=2 * ROWS * D * 900, bytes_accessed=30 << 20, transcendentals=ROWS * CONV),
        name="turn",
    )(sums, mixed, gate, db, xbc, cum, pos, W, gain)


def back_kernel(
    xbc_ref, xdt_ref, dt_ref, cum_ref, sig_ref, dmix_ref, enter_ref, gfresh_ref, ds_ref, ci_ref, pos_ref,
    summ_ref, edge_ref, conv_ref, step_ref, skip_ref,
    din_ref, cgrad_ref, hgrad_ref, dedge_ref,
    state, dacc, posn,
):
    step = pl.program_id(0)

    @pl.when(step == 0)
    def _():
        z = lax.axis_index("ctx")
        start = jnp.zeros((NS, HD), F32)
        for j in (3, 2, 1):
            link = link_of(summ_ref, j)
            start = jnp.where(j > z, start * link + summ_ref[j, 0:NS, :].astype(F32), start)
        state[...] = start
        dacc[LEN : LEN + 8, :] = jnp.zeros((8, CONV), F32)
        posn[LEN : LEN + 8, :] = jnp.zeros((8, 128), F32)
        cgrad_ref[...] = jnp.zeros_like(cgrad_ref)
        hgrad_ref[...] = jnp.zeros_like(hgrad_ref)

    @pl.when(step > 0)
    def _():
        dacc[LEN : LEN + 8, :] = dacc[0:8, :]
        posn[LEN : LEN + 8, :] = posn[0:8, :]

    pos = pos_ref[...]
    posn[0:LEN, :] = pos
    row, lane = iota((LEN, LEN), 0), iota((LEN, LEN), 1)
    gap = (lane - row).astype(F32)
    keep = (gap >= 0) & (gap <= jnp.transpose(pos))
    cum, dt = cum_ref[...], dt_ref[...]
    cum_t = jnp.transpose(cum)
    last = cum[LEN - 1 : LEN]
    pos_last = pos[LEN - 1 : LEN]
    fade = jnp.where(pos > row.astype(F32), jnp.exp2(cum), 0.0)
    ends = jnp.where((LEN - 1) - row.astype(F32) <= pos_last, jnp.exp2(last - cum), 0.0)
    whole = jnp.where(pos_last > LEN - 1, jnp.exp2(last), 0.0)
    basis = xbc_ref[:, HD : HD + NS]
    basis_c = xbc_ref[:, HD + NS : CONV]
    inner = dot_nt(basis, basis_c)
    inner2 = jnp.concatenate([inner, inner], axis=1)
    d_inner = jnp.zeros((LEN, LEN), F32)
    d_b = jnp.zeros((LEN, NS), F32)
    d_c = jnp.zeros((LEN, NS), F32)
    into = jnp.zeros((LEN, 128), F32)
    direct = jnp.zeros((LEN, 128), F32)
    carry = jnp.zeros((LEN, 128), F32)
    later = jnp.zeros((LEN, 128), F32)
    across = jnp.zeros((8, 128), F32)
    sums_t = []
    for p in range(PAIRS):
        lanes = cols(p)
        xs = xbc_ref[:, lanes].astype(F32)
        xdt = xdt_ref[:, lanes]
        dy_wide = dmix_ref[:, lanes]
        dy, dy_low = in_two(dy_wide)
        entered = enter_ref[0, :, lanes]
        after = state[:, lanes]
        after_low = after.astype(BF16)
        dys = stacked(dy)
        spans = []
        for h in (2 * p, 2 * p + 1):
            spans.append(jnp.where(keep, cum_t[h : h + 1, :] - cum[:, h : h + 1], -1e30))
        decays = jnp.exp2(jnp.concatenate(spans, axis=1))
        scores = (decays * inner2).astype(BF16)
        d_scores = dot_nt(twice(xdt), jnp.concatenate([dys, stacked(dy_low)], axis=1)) * decays
        d_inner = d_inner + d_scores[:, :LEN] + d_scores[:, LEN:]
        prod = d_scores * inner2
        sums_t.append(jnp.sum(prod[:, :LEN], axis=0, keepdims=True))
        sums_t.append(jnp.sum(prod[:, LEN:], axis=0, keepdims=True))
        first = jnp.sum(prod[:, :LEN], axis=1, keepdims=True)
        second = jnp.sum(prod[:, LEN:], axis=1, keepdims=True)
        into = into + jnp.where(lane == 2 * p, first, jnp.where(lane == 2 * p + 1, second, 0.0))
        end_pair = spread_heads(ends, p)
        fade_pair = spread_heads(fade, p)
        z_state = dot(basis, after_low) * end_pair
        z = dot(scores, dys) + z_state
        direct = direct + head_sum(xs * z, p)
        later = later + head_sum(xdt.astype(F32) * z_state, p)
        carry = carry + head_sum(dy_wide * dot(basis_c, entered) * fade_pair, p)
        across = across + head_sum(fold8(after * entered.astype(F32)), p)
        d_x = spread_heads(dt, p) * z + skip_ref[:, lanes] * dy_wide
        dacc[0:LEN, lanes] = d_x * ds_ref[:, lanes]
        d_b = d_b + dot_nt(jnp.concatenate(in_two(xdt.astype(F32) * end_pair), axis=1), twice(after_low))
        d_c = d_c + dot_nt(jnp.concatenate(in_two(dy_wide * fade_pair), axis=1), twice(entered))
        state[:, lanes] = after * spread_heads(whole, p) + gfresh_ref[0, :, lanes]
    low = d_inner.astype(BF16)
    d_b = d_b + dot(low, basis_c)
    d_c = d_c + dot_tn(low, basis)
    dacc[0:LEN, HD : HD + NS] = d_b * ds_ref[:, HD : HD + NS]
    dacc[0:LEN, HD + NS : CONV] = d_c * ds_ref[:, HD + NS : CONV]
    out_of = jnp.transpose(jnp.concatenate(sums_t + [jnp.zeros((128 - HEADS, LEN), F32)], axis=0))
    d_rate = (
        dot_full(triangle("suffix"), out_of - into + carry)
        + dot_full(triangle("strict"), later)
        + whole * jnp.sum(across, axis=0, keepdims=True)
    )
    d_step = (direct + d_rate * step_ref[2:3, :]) * sig_ref[...]
    hgrad_ref[0:8, :] += fold8(d_rate * dt)
    hgrad_ref[8:16, :] += fold8(d_step)
    din_ref[:, CONV : CONV + 128] = d_step.astype(BF16)

    for j in range(CONV // 128):
        lanes = cols(j)
        here = dacc[0:LEN, lanes]
        ci = ci_ref[:, lanes].astype(F32)
        d_in = here * conv_ref[3:4, lanes]
        cgrad_ref[24:32, lanes] += fold8(here * ci)
        cgrad_ref[32:40, lanes] += fold8(here)
        for back in (1, 2, 3):
            moved = jnp.where(posn[back : back + LEN, :] >= back, dacc[back : back + LEN, lanes], 0.0)
            d_in = d_in + moved * conv_ref[3 - back : 4 - back, lanes]
            cgrad_ref[8 * (3 - back) : 8 * (3 - back) + 8, lanes] += fold8(moved * ci)
        din_ref[:, lanes] = d_in.astype(BF16)

    @pl.when(step == pl.num_programs(0) - 1)
    def _():
        dacc[8:16, :] = dacc[0:8, :]
        dacc[0:8, :] = jnp.zeros((8, CONV), F32)
        posn[8:16, :] = posn[0:8, :]
        posn[0:8, :] = jnp.zeros((8, 128), F32)
        for j in range(CONV // 128):
            lanes = cols(j)
            ci = edge_ref[:, lanes].astype(F32)[8:16]
            d_in = jnp.zeros((8, 128), F32)
            for back in (1, 2, 3):
                moved = jnp.where(posn[back : back + 8, :] >= back, dacc[back : back + 8, lanes], 0.0)
                d_in = d_in + moved * conv_ref[3 - back : 4 - back, lanes]
                cgrad_ref[8 * (3 - back) : 8 * (3 - back) + 8, lanes] += moved * ci
            dedge_ref[:, lanes] = d_in


def back(xbc, xdt, dt, cum, sig, dmix, entered, gfresh, ds, ci, pos, summs, edge, conv, step, skip):
    top = CHUNKS - 1

    def rows(c):
        return rows_spec(LEN, c, top)

    state = pl.BlockSpec((1, NS, HD), lambda i: (top - i, 0, 0))
    return pl.pallas_call(
        back_kernel,
        grid=(CHUNKS,),
        in_specs=[
            rows(CONV), rows(HD), rows(128), rows(128), rows(128), rows(HD), state, state, rows(CONV), rows(CONV), rows(128),
            whole_spec(4, NS + 16, HD), whole_spec(16, CONV), whole_spec(8, CONV), whole_spec(8, 128), whole_spec(1, HD),
        ],
        out_specs=[rows(CONV + 128), whole_spec(40, CONV), whole_spec(16, 128), whole_spec(8, CONV)],
        out_shape=[
            shape((ROWS, CONV + 128), BF16), shape((40, CONV), F32), shape((16, 128), F32), shape((8, CONV), F32),
        ],
        scratch_shapes=[
            pltpu.VMEM((NS, HD), F32), pltpu.VMEM((LEN + 8, CONV), F32), pltpu.VMEM((LEN + 8, 128), F32),
        ],
        compiler_params=pltpu.CompilerParams(vmem_limit_bytes=56 << 20),
        cost_estimate=pl.CostEstimate(flops=40 * ROWS * HD * 128, bytes_accessed=30 << 20, transcendentals=2 * ROWS * CONV),
        name="back",
    )(xbc, xdt, dt, cum, sig, dmix, entered, gfresh, ds, ci, pos, summs, edge, conv, step, skip)


def rows_kernel(dgate_ref, din_ref, edge_ref, w_ref, x_ref, out_ref, low_ref, ngain_ref):
    step = pl.program_id(0)
    tile = dgate_ref.shape[0]

    @pl.when(step == 0)
    def _():
        ngain_ref[...] = jnp.zeros_like(ngain_ref)

    low_ref[...] = din_ref[...]

    @pl.when((step == pl.num_programs(0) - 1) & (lax.axis_index("ctx") < 3))
    def _():
        tail = din_ref[tile - 16 : tile, 0:CONV].astype(F32)
        more = jnp.concatenate([jnp.zeros((8, CONV), F32), edge_ref[...]], axis=0)
        low_ref[tile - 16 : tile, 0:CONV] = (tail + more).astype(BF16)

    grad = dot_nt(dgate_ref[...], w_ref[:, C_GATE:C_IN]) + dot_nt(low_ref[...], w_ref[:, C_IN:WIDE])
    out_ref[...] = grad.astype(BF16)
    wide = x_ref[...].astype(F32)
    r = lax.rsqrt(jnp.mean(wide * wide, axis=1, keepdims=True) + EPS)
    ngain_ref[...] += fold8(grad * wide * r)


def rows_grad(dgate, din, edge, W, X):
    tile = 256
    return pl.pallas_call(
        rows_kernel,
        grid=(ROWS // tile,),
        in_specs=[
            rows_spec(tile, HD), rows_spec(tile, CONV + 128), whole_spec(8, CONV), whole_spec(D, WIDE), rows_spec(tile, D),
        ],
        out_specs=[rows_spec(tile, D), rows_spec(tile, CONV + 128), whole_spec(8, D)],
        out_shape=[shape((ROWS, D), BF16), shape((ROWS, CONV + 128), BF16), shape((8, D), F32)],
        compiler_params=pltpu.CompilerParams(vmem_limit_bytes=56 << 20),
        cost_estimate=pl.CostEstimate(flops=2 * ROWS * D * 1920, bytes_accessed=20 << 20, transcendentals=0),
        name="rows_grad",
    )(dgate, din, edge, W, X)


def weights_kernel(cot_ref, normed_ref, branch_ref, dgate_ref, din_ref, out_ref):
    normed_t = jnp.transpose(normed_ref[...])
    out_ref[:, C_OUT:C_GATE] = dot(jnp.transpose(cot_ref[...]), branch_ref[...]).astype(BF16)
    out_ref[:, C_GATE:C_IN] = dot(normed_t, dgate_ref[...]).astype(BF16)
    out_ref[:, C_IN:C_MISC] = dot(normed_t, din_ref[:, 0:CONV]).astype(BF16)
    out_ref[:, C_MISC:WIDE] = dot(normed_t, din_ref[:, CONV:]).astype(BF16)


def weights_grad(cot, normed, branch, dgate, din):
    tile = 256
    return pl.pallas_call(
        weights_kernel,
        grid=(D // tile,),
        in_specs=[
            pl.BlockSpec((ROWS, tile), lambda i: (0, i)), pl.BlockSpec((ROWS, tile), lambda i: (0, i)),
            whole_spec(ROWS, HD), whole_spec(ROWS, HD), whole_spec(ROWS, CONV + 128),
        ],
        out_specs=rows_spec(tile, WIDE),
        out_shape=shape((D, WIDE), BF16),
        compiler_params=pltpu.CompilerParams(vmem_limit_bytes=56 << 20),
        cost_estimate=pl.CostEstimate(flops=2 * ROWS * D * WIDE, bytes_accessed=20 << 20, transcendentals=0),
        name="weights_grad",
    )(cot, normed, branch, dgate, din)


def add(a, b):
    return a.astype(F32) + b.astype(F32)


def reduce_kernel(
    g_ref, n_ref, h_ref, gout_ref, nout_ref, yout_ref, hout_ref, hyout_ref,
    G, K, RA, SA, RB, SB, TA, TB, UA, UB, VA, VB, N, M, Q, Y, HZ, HX, HC, HY, ssem, rsem, lsem,
):
    x, c, z, y = place()
    xr, xl, xo = (x + 1) % 4, (x + 3) % 4, (x + 2) % 4
    zr, zl, zo = (z + 1) % 4, (z + 3) % 4, (z + 2) % 4
    yr, yl, yo = (y + 1) % 4, (y + 3) % 4, (y + 2) % 4
    dxr, dxl = device(xr, c, z, y), device(xl, c, z, y)
    dzr, dzl = device(x, c, zr, y), device(x, c, zl, y)
    dyr, dyl, dyo = device(x, c, z, yr), device(x, c, z, yl), device(x, c, z, yo)
    dco = device(x, 1 - c, z, y)
    dxo, dzo = device(xo, c, z, y), device(x, c, zo, y)
    load_g = pltpu.make_async_copy(g_ref, G, lsem.at[0])
    load_g.start()
    load_n = pltpu.make_async_copy(n_ref, N, lsem.at[1])
    load_n.start()
    enter([dxr, dxl, dxo, dzr, dzl, dzo, dyr, dyl, dyo, dco])
    go = Sends(ssem, rsem)
    nA, nB = HALF_A, WIDE - HALF_A
    A, B = pl.ds(0, nA), pl.ds(nA, nB)
    A1, A2 = pl.ds(0, HALF_A1), pl.ds(HALF_A1, nA - HALF_A1)
    B1, B2 = pl.ds(0, HALF_B1 - nA), pl.ds(HALF_B1 - nA, WIDE - HALF_B1)
    H1, H2 = pl.ds(0, 128), pl.ds(128, 128)

    n1 = go(n_ref.at[yo, H1], M.at[0], dyr)
    n2 = go(n_ref.at[yo, H2], M.at[1], dyl)
    HZ[z] = h_ref[...]
    hz = [go(HZ.at[z], HZ.at[z], d) for d in (dzr, dzl, dzo)]
    ka, kb = [], []
    for k in (xo, xr, xl, x):
        ka.append(go(g_ref.at[k, 1 - c, :, :, A], K.at[k, :, :, A], dco))
        j = {0: zo, 1: zr, 2: zl, 3: z}[len(kb)]
        kb.append(go(g_ref.at[:, 1 - c, j, :, B], K.at[:, j, :, B], dco))
    load_g.wait()

    def join_a(k):
        G[k, c, :, :, A] = add(G[k, c, :, :, A], K[k, :, :, A]).astype(BF16)

    def join_b(k):
        G[:, c, k, :, B] = add(G[:, c, k, :, B], K[:, k, :, B]).astype(BF16)

    ga = lambda k, part: G.at[k, c, :, :, part]
    gb = lambda k, part: G.at[:, c, k, :, part]
    GA1, GA2 = pl.ds(0, HALF_A1), pl.ds(HALF_A1, nA - HALF_A1)
    GB1, GB2 = pl.ds(nA, HALF_B1 - nA), pl.ds(HALF_B1, WIDE - HALF_B1)
    ka[0].wait_recv()
    join_a(xo)
    ra1 = go(ga(xo, GA1), RA.at[0, :, :, A1], dxr)
    ra2 = go(ga(xo, GA2), RA.at[0, :, :, A2], dxl)
    kb[0].wait_recv()
    join_b(zo)
    rb1 = go(gb(zo, GB1), RB.at[0, :, :, B1], dzr)
    rb2 = go(gb(zo, GB2), RB.at[0, :, :, B2], dzl)
    for copy in hz:
        copy.wait_recv()
    HX[x] = HZ[0] + HZ[1] + HZ[2] + HZ[3]
    hx = [go(HX.at[x], HX.at[x], d) for d in (dxr, dxl, dxo)]
    ka[1].wait_recv()
    join_a(xr)
    kb[1].wait_recv()
    join_b(zr)
    ka[2].wait_recv()
    join_a(xl)
    kb[2].wait_recv()
    join_b(zl)

    ra1.wait_recv()
    G[xr, c, :, :, GA1] = add(G[xr, c, :, :, GA1], RA[0, :, :, A1]).astype(BF16)
    sa_r = go(ga(xr, A), SA.at[0], dxr)
    rb1.wait_recv()
    G[:, c, zr, :, GB1] = add(G[:, c, zr, :, GB1], RB[0, :, :, B1]).astype(BF16)
    sb_r = go(gb(zr, B), SB.at[0], dzr)
    ra2.wait_recv()
    G[xl, c, :, :, GA2] = add(G[xl, c, :, :, GA2], RA[0, :, :, A2]).astype(BF16)
    sa_l = go(ga(xl, A), SA.at[1], dxl)
    rb2.wait_recv()
    G[:, c, zl, :, GB2] = add(G[:, c, zl, :, GB2], RB[0, :, :, B2]).astype(BF16)
    sb_l = go(gb(zl, B), SB.at[1], dzl)
    ka[3].wait_recv()
    kb[3].wait_recv()

    for copy in hx:
        copy.wait_recv()
    HC[c] = HX[0] + HX[1] + HX[2] + HX[3]
    hc = go(HC.at[c], HC.at[c], dco)
    load_n.wait()
    n1.wait_recv()
    N[yr, H1] = add(N[yr, H1], M[0]).astype(BF16)
    n3 = go(N.at[yr], Q.at[0], dyr)
    n2.wait_recv()
    N[yl, H2] = add(N[yl, H2], M[1]).astype(BF16)
    n4 = go(N.at[yl], Q.at[1], dyl)

    hc.wait_recv()
    HY[y] = HC[0] + HC[1]
    hout_ref[...] = HY[y]
    hy = [go(HY.at[y], HY.at[y], d) for d in (dyr, dyl, dyo)]

    sa_r.wait_recv()
    sa_l.wait_recv()
    own = add(G[x, c, :, :, A], K[x, :, :, A]) + add(SA[0], SA[1])
    TA[...] = own.astype(BF16)
    ta1 = go(TA.at[zo, :, A1], UA.at[:, A1], dzr)
    ta2 = go(TA.at[zo, :, A2], UA.at[:, A2], dzl)
    sb_r.wait_recv()
    sb_l.wait_recv()
    own = add(G[:, c, z, :, B], K[:, z, :, B]) + add(SB[0], SB[1])
    TB[...] = own.astype(BF16)
    tb1 = go(TB.at[xo, :, B1], UB.at[:, B1], dxr)
    tb2 = go(TB.at[xo, :, B2], UB.at[:, B2], dxl)
    ta1.wait_recv()
    TA[zr, :, A1] = add(TA[zr, :, A1], UA[:, A1]).astype(BF16)
    va_r = go(TA.at[zr], VA.at[0], dzr)
    ta2.wait_recv()
    TA[zl, :, A2] = add(TA[zl, :, A2], UA[:, A2]).astype(BF16)
    va_l = go(TA.at[zl], VA.at[1], dzl)
    tb1.wait_recv()
    TB[xr, :, B1] = add(TB[xr, :, B1], UB[:, B1]).astype(BF16)
    vb_r = go(TB.at[xr], VB.at[0], dxr)
    tb2.wait_recv()
    TB[xl, :, B2] = add(TB[xl, :, B2], UB[:, B2]).astype(BF16)
    vb_l = go(TB.at[xl], VB.at[1], dxl)
    vb_r.wait_recv()
    vb_l.wait_recv()
    gout_ref[:, B] = TB[x].astype(F32) + add(VB[0], VB[1])
    Y[y] = gout_ref[:, C_BC:C_MISC]
    ys = [go(Y.at[y], Y.at[y], d) for d in (dyr, dyl, dyo)]
    va_r.wait_recv()
    va_l.wait_recv()
    gout_ref[:, A] = TA[z].astype(F32) + add(VA[0], VA[1])
    for copy in hy:
        copy.wait_recv()
    hyout_ref[...] = HY[0] + HY[1] + HY[2] + HY[3]
    n3.wait_recv()
    n4.wait_recv()
    nout_ref[...] = N[y].astype(F32) + add(Q[0], Q[1])
    for copy in ys:
        copy.wait_recv()
    yout_ref[...] = Y[0] + Y[1] + Y[2] + Y[3]
    go.finish()


def reduce_all(g, n, h):
    nA, nB = HALF_A, WIDE - HALF_A
    return pl.pallas_call(
        reduce_kernel,
        out_shape=(shape((48, WIDE), F32), shape((256, D), F32), shape((48, C_MISC - C_BC), F32), shape((64, 128), F32), shape((64, 128), F32)),
        in_specs=[pl.BlockSpec(memory_space=ANY)] * 2 + [pl.BlockSpec(memory_space=pltpu.VMEM)],
        out_specs=[pl.BlockSpec(memory_space=pltpu.VMEM)] * 5,
        scratch_shapes=[
            pltpu.VMEM((4, 2, 4, 48, WIDE), BF16), pltpu.VMEM((4, 4, 48, WIDE), BF16),
            pltpu.VMEM((1, 4, 48, nA), BF16), pltpu.VMEM((2, 4, 48, nA), BF16),
            pltpu.VMEM((1, 4, 48, nB), BF16), pltpu.VMEM((2, 4, 48, nB), BF16),
            pltpu.VMEM((4, 48, nA), BF16), pltpu.VMEM((4, 48, nB), BF16),
            pltpu.VMEM((48, nA), BF16), pltpu.VMEM((48, nB), BF16),
            pltpu.VMEM((2, 48, nA), BF16), pltpu.VMEM((2, 48, nB), BF16),
            pltpu.VMEM((4, 256, D), BF16), pltpu.VMEM((2, 128, D), BF16), pltpu.VMEM((2, 256, D), BF16),
            pltpu.VMEM((4, 48, C_MISC - C_BC), F32),
            pltpu.VMEM((4, 64, 128), F32), pltpu.VMEM((4, 64, 128), F32), pltpu.VMEM((2, 64, 128), F32),
            pltpu.VMEM((4, 64, 128), F32),
        ] + sems(48),
        compiler_params=comm_params(5, 56 << 20),
        name="reduce_all",
    )(g, n, h)


def after(value, *others):
    return lax.optimization_barrier((value,) + others)[0]


def from_rows(blocks, r, first, count):
    return blocks[:, :r, first : first + count].transpose(1, 0, 2).reshape(r, 32 * count)


def per_device(
    layer_input, out_cotangent, seq_lengths, norm_gain, proj_gate, proj_input, proj_step, proj_state, conv_inner,
    conv_inner_bias, conv_state, conv_state_bias, decay_log, step_bias, skip_scale, gate_gain, proj_out,
):
    ctx = lax.axis_index("ctx")
    tp = lax.axis_index("tp")

    def column(a):
        return jnp.pad(a, ((0, 48 - a.shape[0]), (0, 0)))

    misc = jnp.concatenate(
        [
            proj_step, conv_inner.reshape(48, 2), column(conv_inner_bias), column(gate_gain), column(conv_state),
            column(conv_state_bias[None, :]), norm_gain[:, None], jnp.zeros((48, 93), BF16),
        ],
        axis=1,
    )
    pack = jnp.concatenate([proj_out.T, proj_gate, proj_input, proj_state, misc], axis=1)

    ends = jnp.cumsum(seq_lengths[0])
    token = ctx * ROWS + jnp.arange(ROWS, dtype=jnp.int32)
    begin = jnp.max(jnp.where(token[:, None] >= ends[None, :], ends[None, :], 0), axis=1)
    pos = jnp.broadcast_to((token - begin).astype(F32)[:, None], (ROWS, 128))

    rate = -jnp.exp(decay_log)
    step = jnp.pad(jnp.stack([step_bias, rate * LOG2E, rate]), ((0, 5), (0, 128 - HEADS)))
    skip = jnp.repeat(skip_scale, 64)[None, :]

    W, X, E = gather(pack, layer_input)
    W, X = W.reshape(D, WIDE), X.reshape(ROWS, D)
    cot_own = after(out_cotangent, E)
    cots = [cot_own] + [
        lax.ppermute(cot_own, "tp", [(j, (j + k) % 4) for j in range(4)]) for k in (1, 3, 2)
    ]

    blocks = W[:, C_MISC:].reshape(32, 48, 128).astype(F32)
    conv = jnp.concatenate(
        [
            jnp.concatenate([from_rows(blocks, 48, 12, 2).reshape(4, HD), from_rows(blocks, 4, 18, 8)], axis=1),
            jnp.concatenate([from_rows(blocks, 12, 14, 2).reshape(1, HD), from_rows(blocks, 1, 26, 8)], axis=1),
            jnp.zeros((3, CONV), F32),
        ]
    )
    gain = from_rows(blocks, 12, 16, 2).reshape(1, HD)
    ngain = blocks[:, :, 34].reshape(1, D)

    normed, gate, ci, edge, ds, xbc, xdt, dt, cum, sig, fresh, summ = front(X, W, E, ngain, conv, step, pos)
    summs = swap(summ, "ctx", 1, "swap_state")
    cot_all = jnp.zeros((4, 256, D), BF16)
    for k, part in zip((0, 1, 3, 2), cots):
        cot_all = lax.dynamic_update_slice(cot_all, part[None], ((tp - k) % 4, 0, 0))
    cot_all = cot_all.reshape(ROWS, D)
    mixed, db, sums, entered = scan(xbc, xdt, cum, fresh, gate, pos, summs, cot_all, W, skip, gain)
    sums = swap(sums, "tp", 2, "swap_sums")
    branch, dgate, dmix, out, gfresh, gsumm, tgrad = turn(sums, mixed, gate, db, xbc, cum, pos, W, gain)
    out = out.reshape(4, 256, D)
    out_parts = [lax.dynamic_index_in_dim(out, tp, 0, False)] + [
        lax.ppermute(
            lax.dynamic_index_in_dim(out, (tp + k) % 4, 0, False), "tp", [(j, (j + k) % 4) for j in range(4)]
        )
        for k in (1, 3, 2)
    ]
    gsumms = swap(gsumm, "ctx", 3, "swap_grad")
    din, cgrad, hgrad, dedge = back(
        xbc, xdt, dt, cum, sig, dmix, entered, gfresh, ds, ci, pos, gsumms, edge, conv, step, skip
    )
    dedge, *out_parts = lax.optimization_barrier((dedge, *out_parts))
    dedge = edge_back(dedge, 4)
    ngrad, din, nggrad = rows_grad(dgate, din, dedge, W, X)

    cg = jnp.sum(cgrad.reshape(5, 8, CONV), axis=1)
    tg = jnp.sum(tgrad.reshape(2, 8, HD), axis=1)
    hg = jnp.sum(hgrad.reshape(2, 8, 128), axis=1)
    heads = jnp.stack([hg[0, :HEADS] * rate, hg[1, :HEADS], tg[1].reshape(HEADS, 64).sum(axis=1)])
    heads = jnp.pad(heads, ((0, 3), (0, 128 - HEADS)))
    small = jnp.concatenate(
        [cg.reshape(40, 128), tg[0].reshape(6, 128), jnp.sum(nggrad, axis=0).reshape(12, 128), heads], axis=0
    )
    wgrad = weights_grad(cot_all, normed, branch, dgate, din)
    gsum, share, ysum, plane, every = reduce_all(wgrad.reshape(4, 2, 4, 48, WIDE), ngrad.reshape(4, 256, D), small)

    own = layer_input.astype(F32)
    out_share = sum(part.astype(F32) for part in out_parts)
    layer_output = (own + out_share).astype(BF16)
    scale = lax.rsqrt(jnp.mean(own * own, axis=1, keepdims=True) + EPS)
    weighted = share * ngain
    input_grad = (
        scale * weighted
        - own * (scale * scale * scale) * jnp.mean(own * weighted, axis=1, keepdims=True)
        + out_cotangent.astype(F32)
    )
    block = lax.axis_index("shard") * 4 + ctx
    conv_sum = plane[:40].reshape(5, CONV)[:, :HD].reshape(5, HEADS, 64)
    conv_sum = lax.dynamic_slice_in_dim(conv_sum, block * 2, 2, 2)
    gain_sum = lax.dynamic_slice_in_dim(plane[40:46].reshape(HEADS, 64), block * 2, 2, 1)
    state_sum = lax.dynamic_slice_in_dim(every[:40].reshape(5, CONV)[:, HD:], block * 8 + tp * 2, 2, 1)
    return (
        layer_output,
        input_grad,
        lax.dynamic_slice_in_dim(every[46:58].reshape(D), block * 48 + tp * 12, 12, 0),
        gsum[:, C_GATE:C_IN],
        gsum[:, C_IN:C_BC],
        gsum[:, C_MISC : C_MISC + HEADS],
        lax.dynamic_slice_in_dim(ysum, tp * 12, 12, 0),
        conv_sum[:4],
        conv_sum[4],
        state_sum[:4],
        state_sum[4],
        plane[58, :HEADS],
        plane[59, :HEADS],
        plane[60, :HEADS],
        gain_sum,
        gsum[:, C_OUT:C_GATE].T,
    )


def solution(mesh):
    both = ("shard", "ctx")
    every = ("shard", "ctx", "tp")
    return jax.shard_map(
        per_device,
        mesh=mesh,
        in_specs=(
            P(every, None), P(every, None), P("shard", None), P(both), P(both, "tp"), P(both, "tp"), P(both, "tp"),
            P(both, None), P(None, "tp", both), P("tp", both), P(None, both), P(both), P("tp"), P("tp"), P("tp"),
            P("tp", both), P("tp", both),
        ),
        out_specs=(
            P(every, None), P(every, None), P(every), P(both, "tp"), P(both, "tp"), P(both, "tp"), P(every, None),
            P(None, "tp", both), P("tp", both), P(None, every), P(every), P("tp"), P("tp"), P("tp"), P("tp", both),
            P("tp", both),
        ),
        check_vma=False,
    )
```

time: 1740 us -> 284 us (0.16); the launches traced: 1720 us -> 282 us
  blocking collectives: 881 us -> 0 us
  local copies, waits for them, and re-layouts: 293 us -> 35.5 us
  Pallas kernels: 0 us -> 222 us
  matrix products: 219 us -> 0 us
  other arithmetic: 183 us -> 11.3 us
  starting transfers between devices: 117 us -> 9.12 us
  between operations: 19.4 us -> 1.08 us
    unnamed x4 -> x0, blocking collectives: 603 us -> none
    all_gather x9 -> x0, blocking collectives: 247 us -> none  [the longest x1 47.1 us: per_device(): lax.all_gather(proj_state, ('shard', 'ctx'), axis=0, tiled=True)]
    pallas_call x0 -> x12, Pallas kernels: none -> 222 us  [the longest x1 45 us: reduce_all(): pl.pallas_call(reduce_kernel, out_shape=(shape((48, WIDE), F32), shape((2...]
    dot_general x65 -> x0, matrix products: 217 us -> none  [the longest x12 67 us: block_step(): local_out = jnp.einsum('tsh,shp->thp', scores, inner_x, precision=HIGH)]
    dynamic_update_slice x48 -> x4, local copies, waits for them, and re-layouts: 173 us -> 3.65 us  [per_device(): lax.dynamic_update_slice(cot_all, part[None], ((tp - k) % 4, 0, 0))]
    unnamed x33 -> x0, starting transfers between devices: 111 us -> none
    dynamic_update_slice x24 -> x0, other arithmetic: 44.5 us -> none  [device_outputs(): lax.scan(step_fn, (state_start, seg_before), (inner_x.reshape(blocks, STR...]
    another operation x51 -> x5, other arithmetic: 36.4 us -> 0.8 us  [the longest x2 0.61 us: per_device(): jnp.stack([step_bias, rate * LOG2E, rate])]
  transfers between devices with their start and end apart: 47 -> 6, of which waited for: 0 -> 2; matrix products, arithmetic and copies ran while one was open for 41% -> 5% of each run, Pallas kernels for 0% -> 21%
where the time goes in v1:
time: 284 us; the launch traced here: 282 us
  Pallas kernels  222 us (78%)
  local copies, waits for them, and re-layouts  35.5 us (12%)
  other arithmetic  11.3 us (4%)
  starting transfers between devices  9.12 us (3%)
  waiting for transfers between devices  3.08 us (1%)
    pallas_call x1, Pallas kernels, reduce_all(): pl.pallas_call(reduce_kernel, out_shape=(shape((48, WIDE), F32), shape((2...  45 us
    pallas_call x1, Pallas kernels, gather(): pl.pallas_call(gather_kernel, out_shape=(shape((4, 2, 4, 48, WIDE), BF16)...  43.1 us
    pallas_call x3, Pallas kernels, swap(): pl.pallas_call(functools.partial(swap_kernel, axis), out_shape=shape((4,)...  28.8 us
    pallas_call x1, Pallas kernels, back(): pl.pallas_call(back_kernel, grid=(CHUNKS,), in_specs=[rows(CONV), rows(HD...  25.7 us
    pallas_call x1, Pallas kernels, front(): pl.pallas_call(front_kernel, grid=(ROWS // tile,), in_specs=[rows_spec(ti...  21.9 us
    pallas_call x1, Pallas kernels, weights_grad(): pl.pallas_call(weights_kernel, grid=(D // tile,), in_specs=[pl.BlockSpec(...  14.3 us
    pallas_call x1, Pallas kernels, turn(): pl.pallas_call(turn_kernel, grid=(ROWS // tile,), in_specs=[pl.BlockSpec(...  13.6 us
    pallas_call x1, Pallas kernels, rows_grad(): pl.pallas_call(rows_kernel, grid=(ROWS // tile,), in_specs=[rows_spec(til...  12.7 us
  transfers between devices with their start and end apart: 6, of which 2 were waited for; matrix products, arithmetic and copies ran while one was open for 5% of the time, Pallas kernels for 21%

profile of v1, /device:TPU:0, one launch (start us, length us, event | category | flops | bytes accessed | tf_op | source)
XLA Modules:
  0.0 282.4 jit_solution(16995846061350550568)
XLA Ops:
  1.4 0.7 copy.64
  2.2 0.8 copy.65
  3.1 0.8 copy.68
  3.8 0.8 copy.66
  4.6 0.7 pad.25
  6.0 1.8 concatenate.15.w_ref
  7.7 43.1 %gather_weights.1 = (bf16[4,2,4,48,2688]{4,3,2,1,0:T(8,128)(2,1)}, bf16[4,256,1536]{2,1,0:T(8,128)(2,1)}, bf16[16,1536]{1,0:T(8,128)(2,1)}) custom-call(bf16[48,2688]{1,0:T(8,128)(2,1)} %concatenate.15.w_ref, bf16[256,1536]{1,0:T(8,128)(2,1)} %x_ref.1), custom_call_target="tpu_custom_call" | custom-call | tf_op jit(solution)/shard_map/gather_weights/pallas_call | solution.py:194
  50.8 3.0 %collective-permute-start.2 = (bf16[256,1536]{1,0:T(8,128)(2,1)}, bf16[256,1536]{1,0:T(8,128)(2,1)S(1)}, u32[]{:S(2)}, u32[]{:S(2)}) collective-permute-start(bf16[256,1536]{1,0:T(8,128)(2,1)} %param.18), channel_id=1, source_target_pairs={{0,2},{1,3},{2,0},{3,1},{4,6},{5,7},{6,4},{7,5},{8,10},{9,11},{10,... | collective-permute-start | bytes 2359304 | tf_op jit(solution)/shard_map/ppermute | solution.py:1030
  53.8 1.1 collective-permute-start.1
  54.9 1.0 collective-permute-start
  55.9 1.0 slice.112
  57.9 0.7 reshape_squeeze.9.gain_ref
  60.0 0.7 reshape_reshape.11.gain_ref
  63.0 1.0 broadcast_in_dim.56.pos_ref
  64.0 21.9 %front.1 = (bf16[1024,1536]{1,0:T(8,128)(2,1)}, f32[1024,768]{1,0:T(8,128)}, bf16[1024,1024]{1,0:T(8,128)(2,1)}, bf16[16,1024]{1,0:T(8,128)(2,1)}, f32[1024,1024...) custom-call(bf16[1024,1536]{1,0:T(8,128)(2,1)} %bitcast.112, ...), custom_call_target="tpu_custom_call" | custom-call | flops 6039797760 | bytes 41943040 | tf_op jit(solution)/shard_map/front/pallas_call | solution.py:408
  85.9 12.0 %swap_state.1.summ_ref = bf16[4,144,768]{2,1,0:T(8,128)(2,1)} custom-call(bf16[144,768]{1,0:T(8,128)(2,1)} %get-tuple-element.70.own_ref), custom_call_target="tpu_custom_call" | custom-call | tf_op jit(solution)/shard_map/swap_state/pallas_call | solution.py:232
  98.2 1.2 bitcast_dynamic-update-slice_fusion.3
  99.4 1.2 bitcast_dynamic-update-slice_fusion.2
  100.6 1.2 bitcast_dynamic-update-slice_fusion.1
  101.9 1.7 copy-done
  103.5 12.7 %scan.1 = (f32[1024,768]{1,0:T(8,128)}, f32[1024,768]{1,0:T(8,128)}, f32[64,128]{1,0:T(8,128)}, bf16[8,128,768]{2,1,0:T(8,128)(2,1)}) custom-call(bf16[1024,1024]{1,0:T(8,128)(2,1)} %get-tuple-element.63.xbc_ref, bf16[1024,768]{1,0:T(8,128)(2,1)} %get-tuple-element.64.xdt_ref, f32[1024,128]{1,0:T(8,128)} %get-tuple-element.66.cum_ref, ...), custom_call_target="tpu_custom_call" | custom-call | flops 2831155200 | bytes 31457280 | tf_op jit(solution)/shard_map/scan/pallas_call | solution.py:491
  116.2 6.5 %swap_sums.1.sums_ref = f32[4,64,128]{2,1,0:T(8,128)} custom-call(f32[64,128]{1,0:T(8,128)} %get-tuple-element.72.own_ref), custom_call_target="tpu_custom_call" | custom-call | tf_op jit(solution)/shard_map/swap_sums/pallas_call | solution.py:232
  122.7 13.6 %turn.1 = (bf16[1024,768]{1,0:T(8,128)(2,1)}, bf16[1024,768]{1,0:T(8,128)(2,1)}, f32[1024,768]{1,0:T(8,128)}, bf16[1024,1536]{1,0:T(8,128)(2,1)}, f32[8,128,768]...) custom-call(f32[4,64,128]{2,1,0:T(8,128)} %swap_sums.1.sums_ref, f32[1024,768]{1,0:T(8,128)} %get-tuple-element.73.mixed_ref, ...), custom_call_target="tpu_custom_call" | custom-call | flops 2831155200 | bytes 31457280 | tf_op jit(solution)/shard_map/turn/pallas_call | solution.py:572
  136.3 0.8 bitcast_reduce_fusion.1
  137.3 10.3 %swap_grad.1.summ_ref = bf16[4,144,768]{2,1,0:T(8,128)(2,1)} custom-call(bf16[144,768]{1,0:T(8,128)(2,1)} %get-tuple-element.80.own_ref), custom_call_target="tpu_custom_call" | custom-call | tf_op jit(solution)/shard_map/swap_grad/pallas_call | solution.py:232
  147.7 3.3 %dynamic-slice_bitcast_fusion = (bf16[256,1536]{1,0:T(8,128)(2,1)}, bf16[256,1536]{1,0:T(8,128)(2,1)}, bf16[256,1536]{1,0:T(8,128)(2,1)}, bf16[256,1536]{1,0:T(8,128)(2,1)S(1)}) fusion(bf16[4,256,1536]{2,1,0:T(8,128)(2,1)} %bitcast.96, s32[]{:T(128)S(6)} %select_n.88, s32[]{:T(128)S(6)} %select_n.86, s32[]{:T(128)S(6)} %select_n.84, s32[]{:T(128)S(6)} %select_n.82), kind=kLoop, calls=%fused_computation.15 | loop fusion | bytes 6291472 | tf_op jit(solution)/shard_map/jit(dynamic_index_in_dim)/squeeze | solution.py:1056
  151.0 2.1 collective-permute-start.5
  153.0 1.1 collective-permute-start.4
  154.2 0.9 collective-permute-start.3
  155.1 25.7 %back.1 = (bf16[1024,1152]{1,0:T(8,128)(2,1)}, f32[40,1024]{1,0:T(8,128)}, f32[16,128]{1,0:T(8,128)}, f32[8,1024]{1,0:T(8,128)}) custom-call(bf16[1024,1024]{1,0:T(8,128)(2,1)} %get-tuple-element.63.xbc_ref, bf16[1024,768]{1,0:T(8,128)(2,1)} %get-tuple-element.64.xdt_ref, f32[1024,128]{1,0:T(8,128)} %get-tuple-element.65.dt_ref, ...), custom_call_target="tpu_custom_call" | custom-call | flops 4026531840 | bytes 31457280 | tf_op jit(solution)/shard_map/back/pallas_call | solution.py:735
  180.7 0.7 bitcast_reduce_fusion.2
  181.5 1.0 bitcast_reduce_fusion
  182.5 2.5 collective-permute-done.4
  185.6 4.6 %edge_back.1.edge_ref = f32[8,1024]{1,0:T(8,128)} custom-call(f32[8,1024]{1,0:T(8,128)} %get-tuple-element.92.own_ref), custom_call_target="tpu_custom_call" | custom-call | tf_op jit(solution)/shard_map/edge_back/pallas_call | solution.py:254
  190.2 12.7 %rows_grad.1 = (bf16[1024,1536]{1,0:T(8,128)(2,1)}, bf16[1024,1152]{1,0:T(8,128)(2,1)}, f32[8,1536]{1,0:T(8,128)}) custom-call(bf16[1024,768]{1,0:T(8,128)(2,1)} %get-tuple-element.90.dgate_ref, bf16[1024,1152]{1,0:T(8,128)(2,1)} %get-tuple-element.91.din_ref, f32[8,1024]{1,0:T(8,128)} %edge_back.1.edge_ref, bf16[1536,2688]{1,0:T(8,128)(2,1)} %bitcast.87, ...), custom_call_target="tpu_custom_call" | custom-call | flops 6039797760 | bytes 20971520 | tf_op jit(solution)/shard_map/rows_grad/pallas_call | solution.py:780
  202.9 0.8 reduce_sum.66
  203.7 14.3 %weights_grad.1 = bf16[1536,2688]{1,0:T(8,128)(2,1)} custom-call(bf16[1024,1536]{1,0:T(8,128)(2,1)} %bitcast.94, bf16[1024,1536]{1,0:T(8,128)(2,1)} %get-tuple-element.88.normed_ref, bf16[1024,768]{1,0:T(8,128)(2,1)} %get-tuple-element.89.branch_ref, bf16[1024,768]{1,0:T(8,128)(2,1)} %get-tuple-element.90.dgate_ref, bf16[1024,1152]{1,0:T(8,128)(2,1)} %get-tuple-element.93.din_ref), custom_call_target="tpu_custom_call" | custom-call | flops 8455716864 | bytes 20971520 | tf_op jit(solution)/shard_map/weights_grad/pallas_call | solution.py:804
  218.7 45.0 %reduce_all.1 = (f32[48,2688]{1,0:T(8,128)}, f32[256,1536]{1,0:T(8,128)}, f32[48,256]{1,0:T(8,128)}, f32[64,128]{1,0:T(8,128)}, f32[64,128]{1,0:T(8,128)}) custom-call(bf16[4,2,4,48,2688]{4,3,2,1,0:T(8,128)(2,1)} %bitcast.95, bf16[4,256,1536]{2,1,0:T(8,128)(2,1)} %bitcast.98, f32[64,128]{1,0:T(8,128)} %pad_maximum_fusion.h_ref), custom_call_target="tpu_custom_call" | custom-call | tf_op jit(solution)/shard_map/reduce_all/pallas_call | solution.py:968
  263.7 1.3 slice_bitcast_fusion.2
  265.7 0.7 slice.99
  266.4 0.7 slice_bitcast_fusion.1
  267.1 0.7 slice.103
  268.4 0.7 slice.98
  269.2 1.8 slice_bitcast_fusion
  272.7 0.7 copy.79
  274.7 1.4 constant_dynamic-slice_fusion.4
  276.1 1.8 fusion.1
  278.5 3.9 %fusion.4 = (f32[256,1536]{1,0:T(8,128)}, bf16[256,1536]{1,0:T(8,128)(2,1)}) fusion(bf16[256,1536]{1,0:T(8,128)(2,1)S(1)} %copy-done.1, bf16[256,1536]{1,0:T(8,128)(2,1)} %param.18, f32[256,1536]{1,0:T(8,128)S(1)} %copy-done.2, f32[256]{0:T(256)S(1)} %get-tuple-element.174, f32[256]{0:T(256)S(1)} %get-tuple-element.171, f32[1536]{0:T(1024)S(1)} %mul.90, ...), kind=kLoop, calls=%fused_computation.8 | loop fusion | flops 6684672 | bytes 8659968 | tf_op jit(solution)/shard_map/add | solution.py:1085
  (88 shorter events, 12.7 us)
Async XLA Ops:
  50.8 51.0 %collective-permute-start.2 = (bf16[256,1536]{1,0:T(8,128)(2,1)}, bf16[256,1536]{1,0:T(8,128)(2,1)S(1)}, u32[]{:S(2)}, u32[]{:S(2)}) collective-permute-start(bf16[256,1536]{1,0:T(8,128)(2,1)} %param.18), channel_id=1, source_target_pairs={{0,2},{1,3},{2,0},{3,1},{4,6},{5,7},{6,4},{7,5},{8,10},{9,11},{10,... | collective-permute-start | bytes 2359304 | tf_op jit(solution)/shard_map/ppermute | solution.py:1030
  53.8 46.8 %collective-permute-start.1 = (bf16[256,1536]{1,0:T(8,128)(2,1)}, bf16[256,1536]{1,0:T(8,128)(2,1)}, u32[]{:S(2)}, u32[]{:S(2)}) collective-permute-start(bf16[256,1536]{1,0:T(8,128)(2,1)} %param.18), channel_id=1, source_target_pairs={{0,3},{1,0},{2,1},{3,2},{4,7},{5,4},{6,5},{7,6},{8,11},{9,8},{10,9... | collective-permute-start | bytes 2359304 | tf_op jit(solution)/shard_map/ppermute | solution.py:1030
  54.9 44.5 %collective-permute-start = (bf16[256,1536]{1,0:T(8,128)(2,1)}, bf16[256,1536]{1,0:T(8,128)(2,1)}, u32[]{:S(2)}, u32[]{:S(2)}) collective-permute-start(bf16[256,1536]{1,0:T(8,128)(2,1)} %param.18), channel_id=1, source_target_pairs={{0,1},{1,2},{2,3},{3,0},{4,5},{5,6},{6,7},{7,4},{8,9},{9,10},{10,1... | collective-permute-start | bytes 2359304 | tf_op jit(solution)/shard_map/ppermute | solution.py:1030
  57.4 1.3 copy-start.9
  57.4 1.5 copy-start.10
  57.4 1.6 copy-start.7
  60.0 1.7 copy-start.8
  101.9 1.7 copy-start
  151.0 31.5 %collective-permute-start.5 = (bf16[256,1536]{1,0:T(8,128)(2,1)}, bf16[256,1536]{1,0:T(8,128)(2,1)S(1)}, u32[]{:S(2)}, u32[]{:S(2)}) collective-permute-start(bf16[256,1536]{1,0:T(8,128)(2,1)} %get-tuple-element.156), channel_id=1, source_target_pairs={{0,2},{1,3},{2,0},{3,1},{4,6},{5,7},{6,4},{7,5},{8,10},{9,11},{10,... | collective-permute-start | bytes 2359304 | tf_op jit(solution)/shard_map/ppermute | solution.py:1055
  153.0 32.0 %collective-permute-start.4 = (bf16[256,1536]{1,0:T(8,128)(2,1)}, bf16[256,1536]{1,0:T(8,128)(2,1)S(1)}, u32[]{:S(2)}, u32[]{:S(2)}) collective-permute-start(bf16[256,1536]{1,0:T(8,128)(2,1)} %get-tuple-element.157), channel_id=1, source_target_pairs={{0,3},{1,0},{2,1},{3,2},{4,7},{5,4},{6,5},{7,6},{8,11},{9,8},{10,9... | collective-permute-start | bytes 2359304 | tf_op jit(solution)/shard_map/ppermute | solution.py:1055
  154.2 31.4 %collective-permute-start.3 = (bf16[256,1536]{1,0:T(8,128)(2,1)}, bf16[256,1536]{1,0:T(8,128)(2,1)S(1)}, u32[]{:S(2)}, u32[]{:S(2)}) collective-permute-start(bf16[256,1536]{1,0:T(8,128)(2,1)} %get-tuple-element.158), channel_id=1, source_target_pairs={{0,1},{1,2},{2,3},{3,0},{4,5},{5,6},{6,7},{7,4},{8,9},{9,10},{10,1... | collective-permute-start | bytes 2359304 | tf_op jit(solution)/shard_map/ppermute | solution.py:1055
  182.5 20.4 %copy-start.3 = (bf16[256,1536]{1,0:T(8,128)(2,1)}, bf16[256,1536]{1,0:T(8,128)(2,1)S(1)}, u32[]{:S(2)}) copy-start(bf16[256,1536]{1,0:T(8,128)(2,1)S(1)} %collective-permute-done.5) | copy-start | bytes 2359300
  185.0 17.8 %copy-start.5 = (bf16[256,1536]{1,0:T(8,128)(2,1)}, bf16[256,1536]{1,0:T(8,128)(2,1)S(1)}, u32[]{:S(2)}) copy-start(bf16[256,1536]{1,0:T(8,128)(2,1)S(1)} %collective-permute-done.4) | copy-start | bytes 2359300
  185.6 17.3 %copy-start.6 = (bf16[256,1536]{1,0:T(8,128)(2,1)}, bf16[256,1536]{1,0:T(8,128)(2,1)S(1)}, u32[]{:S(2)}) copy-start(bf16[256,1536]{1,0:T(8,128)(2,1)S(1)} %collective-permute-done.3) | copy-start | bytes 2359300
  263.7 12.5 %copy-start.1 = (bf16[256,1536]{1,0:T(8,128)(2,1)S(1)}, bf16[256,1536]{1,0:T(8,128)(2,1)}, u32[]{:S(2)}) copy-start(bf16[256,1536]{1,0:T(8,128)(2,1)} %x_ref.1) | copy-start | bytes 2359300
  271.0 7.5 %copy-start.2 = (f32[256,1536]{1,0:T(8,128)S(1)}, f32[256,1536]{1,0:T(8,128)}, u32[]{:S(2)}) copy-start(f32[256,1536]{1,0:T(8,128)} %get-tuple-element.99) | copy-start | bytes 4718596
  274.7 3.8 %copy-start.4 = (bf16[256,1536]{1,0:T(8,128)(2,1)S(1)}, bf16[256,1536]{1,0:T(8,128)(2,1)}, u32[]{:S(2)}) copy-start(bf16[256,1536]{1,0:T(8,128)(2,1)} %copy-done.3) | copy-start | bytes 2359300

commit v2 on v1

--- a/solution.py
+++ b/solution.py
@@ -86,6 +86,37 @@
     def finish(self):
         for copy in self.copies:
             copy.wait_send()
+
+
+class Flow:
+    def __init__(self, send_sem, recv_sem):
+        self.send_sem, self.recv_sem, self.known = send_sem, recv_sem, {}
+
+    def add(self, name, src, dst, to):
+        self.known[name] = (len(self.known), src, dst, to)
+
+    def copy(self, name):
+        k, src, dst, to = self.known[name]
+        return pltpu.make_async_remote_copy(
+            src_ref=src(),
+            dst_ref=dst(),
+            send_sem=self.send_sem.at[k],
+            recv_sem=self.recv_sem.at[k],
+            device_id=to,
+            device_id_type=MESH,
+        )
+
+    def start(self, *names):
+        for name in names:
+            self.copy(name).start()
+
+    def wait(self, *names):
+        for name in names:
+            self.copy(name).wait_recv()
+
+    def finish(self):
+        for name in self.known:
+            self.copy(name).wait_send()
 
 
 def sems(n):
@@ -240,28 +271,6 @@
     )(a)
 
 
-def edge_kernel(own_ref, out_ref, ssem, rsem, lsem):
-    x, c, z, y = place()
-    before, after = device(x, c, (z + 3) % 4, y), device(x, c, (z + 1) % 4, y)
-    enter([before, after])
-    go = Sends(ssem, rsem)
-    copy = go(own_ref, out_ref, before)
-    copy.wait_recv()
-    go.finish()
-
-
-def edge_back(a, collective_id):
-    return pl.pallas_call(
-        edge_kernel,
-        out_shape=shape(a.shape, a.dtype),
-        in_specs=[pl.BlockSpec(memory_space=ANY)],
-        out_specs=pl.BlockSpec(memory_space=ANY),
-        scratch_shapes=sems(2),
-        compiler_params=comm_params(collective_id),
-        name="edge_back",
-    )(a)
-
-
 def spread_heads(v, p):
     r = v.shape[0]
     low = jnp.broadcast_to(v[:, 2 * p : 2 * p + 1], (r, 128))
@@ -592,32 +601,285 @@
     )(sums, mixed, gate, db, xbc, cum, pos, W, gain)
 
 
-def back_kernel(
+def add(a, b):
+    return a.astype(F32) + b.astype(F32)
+
+
+class Reduce:
+    def __init__(self, flow, tag, bufs, halves):
+        self.flow, self.tag, self.bufs = flow, tag, bufs
+        G, K, RA, SA, TA, UA, VA, RB, SB, TB, UB, VB = bufs
+        nA, nA1, nB, nB1 = halves
+        self.A, self.B = pl.ds(0, nA), pl.ds(nA, nB)
+        self.A1, self.A2 = pl.ds(0, nA1), pl.ds(nA1, nA - nA1)
+        self.B1, self.B2 = pl.ds(0, nB1), pl.ds(nB1, nB - nB1)
+        self.GB1, self.GB2 = pl.ds(nA, nB1), pl.ds(nA + nB1, nB - nB1)
+        x, c, z, y = place()
+        self.c, self.at = c, (x, z)
+        xr, xl, xo = (x + 1) % 4, (x + 3) % 4, (x + 2) % 4
+        zr, zl, zo = (z + 1) % 4, (z + 3) % 4, (z + 2) % 4
+        self.xs, self.zs = (xr, xl, xo), (zr, zl, zo)
+        dxr, dxl = device(xr, c, z, y), device(xl, c, z, y)
+        dzr, dzl = device(x, c, zr, y), device(x, c, zl, y)
+        A, B, A1, A2, B1, B2, GB1, GB2 = self.A, self.B, self.A1, self.A2, self.B1, self.B2, self.GB1, self.GB2
+
+        def put(name, src, dst, to):
+            flow.add(tag + name, src, dst, to)
+
+        for k in range(4):
+            put("k%d" % k, lambda k=k: G.at[k, 1 - c], lambda k=k: K.at[k], device(x, 1 - c, z, y))
+        put("ra1", lambda: G.at[xo, c, :, :, A1], lambda: RA.at[:, :, A1], dxr)
+        put("ra2", lambda: G.at[xo, c, :, :, A2], lambda: RA.at[:, :, A2], dxl)
+        put("rb1", lambda: G.at[:, c, zo, :, GB1], lambda: RB.at[:, :, B1], dzr)
+        put("rb2", lambda: G.at[:, c, zo, :, GB2], lambda: RB.at[:, :, B2], dzl)
+        put("sar", lambda: G.at[xr, c, :, :, A], lambda: SA.at[0], dxr)
+        put("sal", lambda: G.at[xl, c, :, :, A], lambda: SA.at[1], dxl)
+        put("sbr", lambda: G.at[:, c, zr, :, B], lambda: SB.at[0], dzr)
+        put("sbl", lambda: G.at[:, c, zl, :, B], lambda: SB.at[1], dzl)
+        put("ta1", lambda: TA.at[zo, :, A1], lambda: UA.at[:, A1], dzr)
+        put("ta2", lambda: TA.at[zo, :, A2], lambda: UA.at[:, A2], dzl)
+        put("tb1", lambda: TB.at[xo, :, B1], lambda: UB.at[:, B1], dxr)
+        put("tb2", lambda: TB.at[xo, :, B2], lambda: UB.at[:, B2], dxl)
+        put("var", lambda: TA.at[zr], lambda: VA.at[0], dzr)
+        put("val", lambda: TA.at[zl], lambda: VA.at[1], dzl)
+        put("vbr", lambda: TB.at[xr], lambda: VB.at[0], dxr)
+        put("vbl", lambda: TB.at[xl], lambda: VB.at[1], dxl)
+
+    def start(self, *names):
+        self.flow.start(*[self.tag + name for name in names])
+
+    def wait(self, *names):
+        self.flow.wait(*[self.tag + name for name in names])
+
+    def cores(self, k):
+        self.start("k%d" % k)
+
+    def first(self):
+        G, K = self.bufs[:2]
+        for k in range(4):
+            self.wait("k%d" % k)
+            for j in range(4):
+                G[k, self.c, j] = add(G[k, self.c, j], K[k, j]).astype(BF16)
+        self.start("ra1", "rb1", "ra2", "rb2")
+
+    def second(self):
+        G, K, RA, SA, TA, UA, VA, RB, SB, TB, UB, VB = self.bufs
+        c, (xr, xl, _), (zr, zl, _) = self.c, self.xs, self.zs
+        self.wait("ra1")
+        G[xr, c, :, :, self.A1] = add(G[xr, c, :, :, self.A1], RA[:, :, self.A1]).astype(BF16)
+        self.start("sar")
+        self.wait("rb1")
+        G[:, c, zr, :, self.GB1] = add(G[:, c, zr, :, self.GB1], RB[:, :, self.B1]).astype(BF16)
+        self.start("sbr")
+        self.wait("ra2")
+        G[xl, c, :, :, self.A2] = add(G[xl, c, :, :, self.A2], RA[:, :, self.A2]).astype(BF16)
+        self.start("sal")
+        self.wait("rb2")
+        G[:, c, zl, :, self.GB2] = add(G[:, c, zl, :, self.GB2], RB[:, :, self.B2]).astype(BF16)
+        self.start("sbl")
+
+    def third(self):
+        G, K, RA, SA, TA, UA, VA, RB, SB, TB, UB, VB = self.bufs
+        c, (x, z) = self.c, self.at
+        self.wait("sar", "sal")
+        TA[...] = (G[x, c, :, :, self.A].astype(F32) + add(SA[0], SA[1])).astype(BF16)
+        self.start("ta1", "ta2")
+        self.wait("sbr", "sbl")
+        TB[...] = (G[:, c, z, :, self.B].astype(F32) + add(SB[0], SB[1])).astype(BF16)
+        self.start("tb1", "tb2")
+
+    def fourth(self):
+        G, K, RA, SA, TA, UA, VA, RB, SB, TB, UB, VB = self.bufs
+        (xr, xl, _), (zr, zl, _) = self.xs, self.zs
+        self.wait("ta1")
+        TA[zr, :, self.A1] = add(TA[zr, :, self.A1], UA[:, self.A1]).astype(BF16)
+        self.start("var")
+        self.wait("ta2")
+        TA[zl, :, self.A2] = add(TA[zl, :, self.A2], UA[:, self.A2]).astype(BF16)
+        self.start("val")
+        self.wait("tb1")
+        TB[xr, :, self.B1] = add(TB[xr, :, self.B1], UB[:, self.B1]).astype(BF16)
+        self.start("vbr")
+        self.wait("tb2")
+        TB[xl, :, self.B2] = add(TB[xl, :, self.B2], UB[:, self.B2]).astype(BF16)
+        self.start("vbl")
+
+    def last(self, out_ref):
+        G, K, RA, SA, TA, UA, VA, RB, SB, TB, UB, VB = self.bufs
+        x, z = self.at
+        self.wait("vbr", "vbl")
+        out_ref[:, self.B] = TB[x].astype(F32) + add(VB[0], VB[1])
+        self.wait("var", "val")
+        out_ref[:, self.A] = TA[z].astype(F32) + add(VA[0], VA[1])
+
+
+def reduce_bufs(halves):
+    nA, nA1, nB, nB1 = halves
+
+    def half(n):
+        return [
+            pltpu.VMEM((4, 48, n), BF16), pltpu.VMEM((2, 4, 48, n), BF16), pltpu.VMEM((4, 48, n), BF16),
+            pltpu.VMEM((48, n), BF16), pltpu.VMEM((2, 48, n), BF16),
+        ]
+
+    return [pltpu.VMEM((4, 2, 4, 48, nA + nB), BF16), pltpu.VMEM((4, 4, 48, nA + nB), BF16)] + half(nA) + half(nB)
+
+
+class RowSum:
+    def __init__(self, flow, tag, N, M, Q, first_from=None):
+        self.flow, self.tag, self.bufs = flow, tag, (N, M, Q)
+        x, c, z, y = place()
+        self.yr, self.yl, self.yo, self.y = (y + 1) % 4, (y + 3) % 4, (y + 2) % 4, y
+        right, left = device(x, c, z, self.yr), device(x, c, z, self.yl)
+        source = N if first_from is None else first_from
+        self.h1, self.h2 = pl.ds(0, 128), pl.ds(128, 128)
+        flow.add(tag + "1", lambda: source.at[self.yo, self.h1], lambda: M.at[0], right)
+        flow.add(tag + "2", lambda: source.at[self.yo, self.h2], lambda: M.at[1], left)
+        flow.add(tag + "3", lambda: N.at[self.yr], lambda: Q.at[0], right)
+        flow.add(tag + "4", lambda: N.at[self.yl], lambda: Q.at[1], left)
+
+    def first(self):
+        self.flow.start(self.tag + "1", self.tag + "2")
+
+    def second(self):
+        N, M, Q = self.bufs
+        self.flow.wait(self.tag + "1")
+        N[self.yr, self.h1] = add(N[self.yr, self.h1], M[0]).astype(BF16)
+        self.flow.start(self.tag + "3")
+        self.flow.wait(self.tag + "2")
+        N[self.yl, self.h2] = add(N[self.yl, self.h2], M[1]).astype(BF16)
+        self.flow.start(self.tag + "4")
+
+    def last(self, out_ref):
+        N, M, Q = self.bufs
+        self.flow.wait(self.tag + "3", self.tag + "4")
+        out_ref[...] = N[self.y].astype(F32) + add(Q[0], Q[1])
+
+
+def row_bufs():
+    return [pltpu.VMEM((4, 256, D), BF16), pltpu.VMEM((2, 128, D), BF16), pltpu.VMEM((2, 256, D), BF16)]
+
+
+MID = (768, 384, 768, 384)
+TAIL = (640, 384, 512, 256)
+PRE = 4
+
+
+def middle_kernel(
+    gsumm_ref, out_ref, cot_ref, normed_ref, branch_ref, dgate_ref,
     xbc_ref, xdt_ref, dt_ref, cum_ref, sig_ref, dmix_ref, enter_ref, gfresh_ref, ds_ref, ci_ref, pos_ref,
-    summ_ref, edge_ref, conv_ref, step_ref, skip_ref,
-    din_ref, cgrad_ref, hgrad_ref, dedge_ref,
-    state, dacc, posn,
+    edge_ref, conv_ref, step_ref, skip_ref,
+    din_ref, cgrad_ref, hgrad_ref, dedge_ref, gout_ref, share_ref,
+    state, dacc, posn, summ, edge_out, edge_in, *rest,
 ):
+    bufs, (N, M, Q, ssem, rsem, lsem) = rest[:-6], rest[-6:]
     step = pl.program_id(0)
+    steps = PRE + CHUNKS
+    x, c, z, y = place()
+    flow = Flow(ssem, rsem)
+    reduce = Reduce(flow, "g", bufs, MID)
+    rows = RowSum(flow, "n", N, M, Q, out_ref)
+    others_z = [device(x, c, (z + k) % 4, y) for k in (1, 3, 2)]
+    for k in range(3):
+        flow.add("s%d" % k, lambda: gsumm_ref, lambda: summ.at[z], others_z[k])
+    flow.add("e", lambda: edge_out, lambda: edge_in, others_z[1])
+    load_n = pltpu.make_async_copy(out_ref, N, lsem.at[0])
+    load_s = pltpu.make_async_copy(gsumm_ref, summ.at[z], lsem.at[1])
 
     @pl.when(step == 0)
     def _():
-        z = lax.axis_index("ctx")
+        load_s.start()
+        load_n.start()
+        enter(
+            others_z
+            + [device((x + 1) % 4, c, z, y), device((x + 3) % 4, c, z, y)]
+            + [device(x, c, z, (y + 1) % 4), device(x, c, z, (y + 3) % 4), device(x, 1 - c, z, y)]
+        )
+        flow.start("s0", "s1", "s2")
+        rows.first()
+
+    for k in range(PRE):
+
+        @pl.when(step == k)
+        def _():
+            G = bufs[0]
+            out = dot(jnp.transpose(cot_ref[...]), branch_ref[...]).astype(BF16)
+            gate = dot(jnp.transpose(normed_ref[...]), dgate_ref[...]).astype(BF16)
+            G[k, :, :, :, 0:HD] = out.reshape(2, 4, 48, HD)
+            G[k, :, :, :, HD : 2 * HD] = gate.reshape(2, 4, 48, HD)
+            reduce.cores(k)
+
+    @pl.when(step == PRE)
+    def _():
+        flow.wait("s0", "s1", "s2")
+        load_s.wait()
         start = jnp.zeros((NS, HD), F32)
         for j in (3, 2, 1):
-            link = link_of(summ_ref, j)
-            start = jnp.where(j > z, start * link + summ_ref[j, 0:NS, :].astype(F32), start)
+            link = link_of(summ, j)
+            start = jnp.where(j > z, start * link + summ[j, 0:NS, :].astype(F32), start)
         state[...] = start
         dacc[LEN : LEN + 8, :] = jnp.zeros((8, CONV), F32)
         posn[LEN : LEN + 8, :] = jnp.zeros((8, 128), F32)
         cgrad_ref[...] = jnp.zeros_like(cgrad_ref)
         hgrad_ref[...] = jnp.zeros_like(hgrad_ref)
-
-    @pl.when(step > 0)
+        reduce.first()
+
+    @pl.when(step == PRE + 1)
+    def _():
+        load_n.wait()
+        rows.second()
+
+    @pl.when(step == PRE + 2)
+    def _():
+        reduce.second()
+
+    @pl.when(step == PRE + 5)
+    def _():
+        reduce.third()
+
+    @pl.when(step == PRE + 6)
+    def _():
+        reduce.fourth()
+
+    @pl.when(step > PRE)
     def _():
         dacc[LEN : LEN + 8, :] = dacc[0:8, :]
         posn[LEN : LEN + 8, :] = posn[0:8, :]
 
+    @pl.when(step >= PRE)
+    def _():
+        back_chunk(
+            xbc_ref, xdt_ref, dt_ref, cum_ref, sig_ref, dmix_ref, enter_ref, gfresh_ref, ds_ref, ci_ref, pos_ref,
+            conv_ref, step_ref, skip_ref, din_ref, cgrad_ref, hgrad_ref, state, dacc, posn,
+        )
+
+    @pl.when(step == steps - 1)
+    def _():
+        dacc[8:16, :] = dacc[0:8, :]
+        dacc[0:8, :] = jnp.zeros((8, CONV), F32)
+        posn[8:16, :] = posn[0:8, :]
+        posn[0:8, :] = jnp.zeros((8, 128), F32)
+        for j in range(CONV // 128):
+            lanes = cols(j)
+            ci = edge_ref[:, lanes].astype(F32)[8:16]
+            d_in = jnp.zeros((8, 128), F32)
+            for back in (1, 2, 3):
+                moved = jnp.where(posn[back : back + 8, :] >= back, dacc[back : back + 8, lanes], 0.0)
+                d_in = d_in + moved * conv_ref[3 - back : 4 - back, lanes]
+                cgrad_ref[8 * (3 - back) : 8 * (3 - back) + 8, lanes] += moved * ci
+            edge_out[:, lanes] = d_in
+        flow.start("e")
+        reduce.last(gout_ref)
+        rows.last(share_ref)
+        flow.wait("e")
+        dedge_ref[...] = edge_in[...]
+        flow.finish()
+
+
+def back_chunk(
+    xbc_ref, xdt_ref, dt_ref, cum_ref, sig_ref, dmix_ref, enter_ref, gfresh_ref, ds_ref, ci_ref, pos_ref,
+    conv_ref, step_ref, skip_ref, din_ref, cgrad_ref, hgrad_ref, state, dacc, posn,
+):
     pos = pos_ref[...]
     posn[0:LEN, :] = pos
     row, lane = iota((LEN, LEN), 0), iota((LEN, LEN), 1)
@@ -708,283 +970,196 @@
             cgrad_ref[8 * (3 - back) : 8 * (3 - back) + 8, lanes] += fold8(moved * ci)
         din_ref[:, lanes] = d_in.astype(BF16)
 
-    @pl.when(step == pl.num_programs(0) - 1)
-    def _():
-        dacc[8:16, :] = dacc[0:8, :]
-        dacc[0:8, :] = jnp.zeros((8, CONV), F32)
-        posn[8:16, :] = posn[0:8, :]
-        posn[0:8, :] = jnp.zeros((8, 128), F32)
-        for j in range(CONV // 128):
-            lanes = cols(j)
-            ci = edge_ref[:, lanes].astype(F32)[8:16]
-            d_in = jnp.zeros((8, 128), F32)
-            for back in (1, 2, 3):
-                moved = jnp.where(posn[back : back + 8, :] >= back, dacc[back : back + 8, lanes], 0.0)
-                d_in = d_in + moved * conv_ref[3 - back : 4 - back, lanes]
-                cgrad_ref[8 * (3 - back) : 8 * (3 - back) + 8, lanes] += moved * ci
-            dedge_ref[:, lanes] = d_in
-
-
-def back(xbc, xdt, dt, cum, sig, dmix, entered, gfresh, ds, ci, pos, summs, edge, conv, step, skip):
+
+def middle(
+    gsumm, out, cot, normed, branch, dgate, xbc, xdt, dt, cum, sig, dmix, entered, gfresh, ds, ci, pos, edge, conv, step, skip
+):
     top = CHUNKS - 1
 
+    def chunk(i):
+        return jnp.minimum(top + PRE - i, top)
+
     def rows(c):
-        return rows_spec(LEN, c, top)
-
-    state = pl.BlockSpec((1, NS, HD), lambda i: (top - i, 0, 0))
+        return pl.BlockSpec((LEN, c), lambda i: (chunk(i), 0))
+
+    def tiles():
+        return pl.BlockSpec((ROWS, D // PRE), lambda i: (0, jnp.minimum(i, PRE - 1)))
+
+    state = pl.BlockSpec((1, NS, HD), lambda i: (chunk(i), 0, 0))
+    anywhere = pl.BlockSpec(memory_space=ANY)
     return pl.pallas_call(
-        back_kernel,
-        grid=(CHUNKS,),
+        middle_kernel,
+        grid=(PRE + CHUNKS,),
         in_specs=[
+            anywhere, anywhere, tiles(), tiles(), whole_spec(ROWS, HD), whole_spec(ROWS, HD),
             rows(CONV), rows(HD), rows(128), rows(128), rows(128), rows(HD), state, state, rows(CONV), rows(CONV), rows(128),
-            whole_spec(4, NS + 16, HD), whole_spec(16, CONV), whole_spec(8, CONV), whole_spec(8, 128), whole_spec(1, HD),
-        ],
-        out_specs=[rows(CONV + 128), whole_spec(40, CONV), whole_spec(16, 128), whole_spec(8, CONV)],
+            whole_spec(16, CONV), whole_spec(8, CONV), whole_spec(8, 128), whole_spec(1, HD),
+        ],
+        out_specs=[
+            rows(CONV + 128), whole_spec(40, CONV), whole_spec(16, 128), whole_spec(8, CONV), whole_spec(48, 2 * HD),
+            whole_spec(256, D),
+        ],
         out_shape=[
             shape((ROWS, CONV + 128), BF16), shape((40, CONV), F32), shape((16, 128), F32), shape((8, CONV), F32),
+            shape((48, 2 * HD), F32), shape((256, D), F32),
         ],
         scratch_shapes=[
             pltpu.VMEM((NS, HD), F32), pltpu.VMEM((LEN + 8, CONV), F32), pltpu.VMEM((LEN + 8, 128), F32),
-        ],
-        compiler_params=pltpu.CompilerParams(vmem_limit_bytes=56 << 20),
+            pltpu.VMEM((4, NS + 16, HD), BF16), pltpu.VMEM((8, CONV), F32), pltpu.VMEM((8, CONV), F32),
+        ] + reduce_bufs(MID) + row_bufs() + sems(32),
+        compiler_params=comm_params(3, 60 << 20),
         cost_estimate=pl.CostEstimate(flops=40 * ROWS * HD * 128, bytes_accessed=30 << 20, transcendentals=2 * ROWS * CONV),
-        name="back",
-    )(xbc, xdt, dt, cum, sig, dmix, entered, gfresh, ds, ci, pos, summs, edge, conv, step, skip)
-
-
-def rows_kernel(dgate_ref, din_ref, edge_ref, w_ref, x_ref, out_ref, low_ref, ngain_ref):
-    step = pl.program_id(0)
-    tile = dgate_ref.shape[0]
-
-    @pl.when(step == 0)
-    def _():
-        ngain_ref[...] = jnp.zeros_like(ngain_ref)
-
-    low_ref[...] = din_ref[...]
-
-    @pl.when((step == pl.num_programs(0) - 1) & (lax.axis_index("ctx") < 3))
-    def _():
-        tail = din_ref[tile - 16 : tile, 0:CONV].astype(F32)
-        more = jnp.concatenate([jnp.zeros((8, CONV), F32), edge_ref[...]], axis=0)
-        low_ref[tile - 16 : tile, 0:CONV] = (tail + more).astype(BF16)
-
-    grad = dot_nt(dgate_ref[...], w_ref[:, C_GATE:C_IN]) + dot_nt(low_ref[...], w_ref[:, C_IN:WIDE])
-    out_ref[...] = grad.astype(BF16)
-    wide = x_ref[...].astype(F32)
-    r = lax.rsqrt(jnp.mean(wide * wide, axis=1, keepdims=True) + EPS)
-    ngain_ref[...] += fold8(grad * wide * r)
-
-
-def rows_grad(dgate, din, edge, W, X):
-    tile = 256
+        name="middle",
+    )(gsumm, out, cot, normed, branch, dgate, xbc, xdt, dt, cum, sig, dmix, entered, gfresh, ds, ci, pos, edge, conv, step, skip)
+
+
+def tail_kernel(
+    dgate_ref, din_ref, w_ref, x_ref, normed_ref, edge_ref, cgrad_ref, tgrad_ref, hgrad_ref,
+    gout_ref, share_ref, ysum_ref, plane_ref, every_ref,
+    dgate, din, w, xs, normed, small, HZ, HX, HC, HY, Y, *rest,
+):
+    bufs, (N, M, Q, ssem, rsem, lsem) = rest[:-6], rest[-6:]
+    x, c, z, y = place()
+    xs_other = [device((x + k) % 4, c, z, y) for k in (1, 3, 2)]
+    zs_other = [device(x, c, (z + k) % 4, y) for k in (1, 3, 2)]
+    ys_other = [device(x, c, z, (y + k) % 4) for k in (1, 3, 2)]
+    core = device(x, 1 - c, z, y)
+    loads = [
+        pltpu.make_async_copy(src, dst, lsem.at[k])
+        for k, (src, dst) in enumerate(
+            [(w_ref.at[:, C_GATE:WIDE], w), (dgate_ref, dgate), (din_ref, din), (x_ref, xs), (normed_ref, normed)]
+        )
+    ]
+    for load in loads:
+        load.start()
+    enter(xs_other + zs_other + ys_other + [core])
+    flow = Flow(ssem, rsem)
+    reduce = Reduce(flow, "g", bufs, TAIL)
+    rows = RowSum(flow, "n", N, M, Q)
+    for k in range(3):
+        flow.add("hz%d" % k, lambda: HZ.at[z], lambda: HZ.at[z], zs_other[k])
+        flow.add("hx%d" % k, lambda: HX.at[x], lambda: HX.at[x], xs_other[k])
+        flow.add("hy%d" % k, lambda: HY.at[y], lambda: HY.at[y], ys_other[k])
+        flow.add("y%d" % k, lambda: Y.at[y], lambda: Y.at[y], ys_other[k])
+    flow.add("hc", lambda: HC.at[c], lambda: HC.at[c], core)
+
+    for load in loads[:3]:
+        load.wait()
+    end = din[ROWS - 16 : ROWS, 0:CONV].astype(F32)
+    more = jnp.concatenate([jnp.zeros((8, CONV), F32), edge_ref[...]], axis=0)
+    din[ROWS - 16 : ROWS, 0:CONV] = (end + more).astype(BF16)
+
+    for k in range(40):
+        j = k % 8
+        small[k : k + 1, :] = jnp.sum(cgrad_ref[8 * (k // 8) : 8 * (k // 8) + 8, cols(j)], axis=0, keepdims=True)
+    for j in range(6):
+        small[40 + j : 41 + j, :] = jnp.sum(tgrad_ref[0:8, cols(j)], axis=0, keepdims=True)
+        small[58 + j : 59 + j, :] = jnp.sum(tgrad_ref[8:16, cols(j)], axis=0, keepdims=True)
+    small[64:65, :] = jnp.sum(hgrad_ref[0:8, :], axis=0, keepdims=True)
+    small[65:66, :] = jnp.sum(hgrad_ref[8:16, :], axis=0, keepdims=True)
+    small[66:72, :] = jnp.zeros((6, 128), F32)
+
+    gains = jnp.zeros((8, D), F32)
+    for k, block in enumerate((rows.yo, rows.yr, rows.yl, rows.y)):
+        here = pl.ds(pl.multiple_of(block * 256, 256), 256)
+        grad = dot_nt(dgate[here, :], w[:, 0:HD]) + dot_nt(din[here, :], w[:, HD : WIDE - C_GATE])
+        N[block] = grad.astype(BF16)
+        if k == 0:
+            rows.first()
+            loads[3].wait()
+        wide = xs[here, :].astype(F32)
+        r = lax.rsqrt(jnp.mean(wide * wide, axis=1, keepdims=True) + EPS)
+        gains = gains + fold8(grad * wide * r)
+    gains = jnp.sum(gains, axis=0, keepdims=True)
+    for j in range(12):
+        small[46 + j : 47 + j, :] = gains[:, cols(j)]
+    HZ[z] = small[...]
+    flow.start("hz0", "hz1", "hz2")
+    loads[4].wait()
+    G = bufs[0]
+    for k in range(4):
+        part = dot(jnp.transpose(normed[:, 384 * k : 384 * k + 384]), din[...]).astype(BF16)
+        G[k] = part.reshape(2, 4, 48, CONV + 128)
+        reduce.cores(k)
+        if k == 0:
+            rows.second()
+    flow.wait("hz0", "hz1", "hz2")
+    HX[x] = HZ[0] + HZ[1] + HZ[2] + HZ[3]
+    flow.start("hx0", "hx1", "hx2")
+    reduce.first()
+    flow.wait("hx0", "hx1", "hx2")
+    HC[c] = HX[0] + HX[1] + HX[2] + HX[3]
+    flow.start("hc")
+    reduce.second()
+    flow.wait("hc")
+    total = HC[0] + HC[1]
+    HY[y] = total
+    plane_ref[...] = total
+    flow.start("hy0", "hy1", "hy2")
+    reduce.third()
+    flow.wait("hy0", "hy1", "hy2")
+    every_ref[...] = HY[0] + HY[1] + HY[2] + HY[3]
+    reduce.fourth()
+    reduce.last(gout_ref)
+    Y[y] = gout_ref[:, HD:CONV]
+    flow.start("y0", "y1", "y2")
+    rows.last(share_ref)
+    flow.wait("y0", "y1", "y2")
+    ysum_ref[...] = Y[0] + Y[1] + Y[2] + Y[3]
+    flow.finish()
+
+
+def tail(dgate, din, W, X, normed, edge, cgrad, tgrad, hgrad):
+    vmem = pl.BlockSpec(memory_space=pltpu.VMEM)
+    table = pltpu.VMEM((4, 72, 128), F32)
     return pl.pallas_call(
-        rows_kernel,
-        grid=(ROWS // tile,),
-        in_specs=[
-            rows_spec(tile, HD), rows_spec(tile, CONV + 128), whole_spec(8, CONV), whole_spec(D, WIDE), rows_spec(tile, D),
-        ],
-        out_specs=[rows_spec(tile, D), rows_spec(tile, CONV + 128), whole_spec(8, D)],
-        out_shape=[shape((ROWS, D), BF16), shape((ROWS, CONV + 128), BF16), shape((8, D), F32)],
-        compiler_params=pltpu.CompilerParams(vmem_limit_bytes=56 << 20),
-        cost_estimate=pl.CostEstimate(flops=2 * ROWS * D * 1920, bytes_accessed=20 << 20, transcendentals=0),
-        name="rows_grad",
-    )(dgate, din, edge, W, X)
-
-
-def weights_kernel(cot_ref, normed_ref, branch_ref, dgate_ref, din_ref, out_ref):
-    normed_t = jnp.transpose(normed_ref[...])
-    out_ref[:, C_OUT:C_GATE] = dot(jnp.transpose(cot_ref[...]), branch_ref[...]).astype(BF16)
-    out_ref[:, C_GATE:C_IN] = dot(normed_t, dgate_ref[...]).astype(BF16)
-    out_ref[:, C_IN:C_MISC] = dot(normed_t, din_ref[:, 0:CONV]).astype(BF16)
-    out_ref[:, C_MISC:WIDE] = dot(normed_t, din_ref[:, CONV:]).astype(BF16)
-
-
-def weights_grad(cot, normed, branch, dgate, din):
-    tile = 256
+        tail_kernel,
+        out_shape=(
+            shape((48, CONV + 128), F32), shape((256, D), F32), shape((48, 2 * NS), F32), shape((72, 128), F32),
+            shape((72, 128), F32),
+        ),
+        in_specs=[pl.BlockSpec(memory_space=ANY)] * 5 + [vmem] * 4,
+        out_specs=[vmem] * 5,
+        scratch_shapes=[
+            pltpu.VMEM((ROWS, HD), BF16), pltpu.VMEM((ROWS, CONV + 128), BF16), pltpu.VMEM((D, WIDE - C_GATE), BF16),
+            pltpu.VMEM((ROWS, D), BF16), pltpu.VMEM((ROWS, D), BF16), pltpu.VMEM((72, 128), F32),
+            table, table, pltpu.VMEM((2, 72, 128), F32), table, pltpu.VMEM((4, 48, 2 * NS), F32),
+        ] + reduce_bufs(TAIL) + row_bufs() + [
+            pltpu.SemaphoreType.DMA((48,)), pltpu.SemaphoreType.DMA((48,)), pltpu.SemaphoreType.DMA((8,)),
+        ],
+        compiler_params=comm_params(5, 60 << 20),
+        name="tail",
+    )(dgate, din, W, X, normed, edge, cgrad, tgrad, hgrad)
+
+
+def finish_kernel(
+    x_ref, cot_ref, out_ref, share_ref, gain_ref, mid_ref, tail_ref, ysum_ref,
+    lout_ref, grad_ref, gate_ref, in_ref, wout_ref, bc_ref,
+):
+    own = x_ref[...].astype(F32)
+    lout_ref[...] = (own + out_ref[...]).astype(BF16)
+    scale = lax.rsqrt(jnp.mean(own * own, axis=1, keepdims=True) + EPS)
+    weighted = share_ref[...] * gain_ref[...]
+    slope = scale * scale * scale * jnp.mean(own * weighted, axis=1, keepdims=True)
+    grad_ref[...] = scale * weighted - own * slope + cot_ref[...].astype(F32)
+    gate_ref[...] = mid_ref[:, HD : 2 * HD]
+    in_ref[...] = tail_ref[:, 0:HD]
+    wout_ref[...] = jnp.transpose(mid_ref[:, 0:HD])
+    bc_ref[...] = ysum_ref[...]
+
+
+def finish(rows, cot, out, share, gain, mid, tail, ysum):
     return pl.pallas_call(
-        weights_kernel,
-        grid=(D // tile,),
-        in_specs=[
-            pl.BlockSpec((ROWS, tile), lambda i: (0, i)), pl.BlockSpec((ROWS, tile), lambda i: (0, i)),
-            whole_spec(ROWS, HD), whole_spec(ROWS, HD), whole_spec(ROWS, CONV + 128),
-        ],
-        out_specs=rows_spec(tile, WIDE),
-        out_shape=shape((D, WIDE), BF16),
-        compiler_params=pltpu.CompilerParams(vmem_limit_bytes=56 << 20),
-        cost_estimate=pl.CostEstimate(flops=2 * ROWS * D * WIDE, bytes_accessed=20 << 20, transcendentals=0),
-        name="weights_grad",
-    )(cot, normed, branch, dgate, din)
-
-
-def add(a, b):
-    return a.astype(F32) + b.astype(F32)
-
-
-def reduce_kernel(
-    g_ref, n_ref, h_ref, gout_ref, nout_ref, yout_ref, hout_ref, hyout_ref,
-    G, K, RA, SA, RB, SB, TA, TB, UA, UB, VA, VB, N, M, Q, Y, HZ, HX, HC, HY, ssem, rsem, lsem,
-):
-    x, c, z, y = place()
-    xr, xl, xo = (x + 1) % 4, (x + 3) % 4, (x + 2) % 4
-    zr, zl, zo = (z + 1) % 4, (z + 3) % 4, (z + 2) % 4
-    yr, yl, yo = (y + 1) % 4, (y + 3) % 4, (y + 2) % 4
-    dxr, dxl = device(xr, c, z, y), device(xl, c, z, y)
-    dzr, dzl = device(x, c, zr, y), device(x, c, zl, y)
-    dyr, dyl, dyo = device(x, c, z, yr), device(x, c, z, yl), device(x, c, z, yo)
-    dco = device(x, 1 - c, z, y)
-    dxo, dzo = device(xo, c, z, y), device(x, c, zo, y)
-    load_g = pltpu.make_async_copy(g_ref, G, lsem.at[0])
-    load_g.start()
-    load_n = pltpu.make_async_copy(n_ref, N, lsem.at[1])
-    load_n.start()
-    enter([dxr, dxl, dxo, dzr, dzl, dzo, dyr, dyl, dyo, dco])
-    go = Sends(ssem, rsem)
-    nA, nB = HALF_A, WIDE - HALF_A
-    A, B = pl.ds(0, nA), pl.ds(nA, nB)
-    A1, A2 = pl.ds(0, HALF_A1), pl.ds(HALF_A1, nA - HALF_A1)
-    B1, B2 = pl.ds(0, HALF_B1 - nA), pl.ds(HALF_B1 - nA, WIDE - HALF_B1)
-    H1, H2 = pl.ds(0, 128), pl.ds(128, 128)
-
-    n1 = go(n_ref.at[yo, H1], M.at[0], dyr)
-    n2 = go(n_ref.at[yo, H2], M.at[1], dyl)
-    HZ[z] = h_ref[...]
-    hz = [go(HZ.at[z], HZ.at[z], d) for d in (dzr, dzl, dzo)]
-    ka, kb = [], []
-    for k in (xo, xr, xl, x):
-        ka.append(go(g_ref.at[k, 1 - c, :, :, A], K.at[k, :, :, A], dco))
-        j = {0: zo, 1: zr, 2: zl, 3: z}[len(kb)]
-        kb.append(go(g_ref.at[:, 1 - c, j, :, B], K.at[:, j, :, B], dco))
-    load_g.wait()
-
-    def join_a(k):
-        G[k, c, :, :, A] = add(G[k, c, :, :, A], K[k, :, :, A]).astype(BF16)
-
-    def join_b(k):
-        G[:, c, k, :, B] = add(G[:, c, k, :, B], K[:, k, :, B]).astype(BF16)
-
-    ga = lambda k, part: G.at[k, c, :, :, part]
-    gb = lambda k, part: G.at[:, c, k, :, part]
-    GA1, GA2 = pl.ds(0, HALF_A1), pl.ds(HALF_A1, nA - HALF_A1)
-    GB1, GB2 = pl.ds(nA, HALF_B1 - nA), pl.ds(HALF_B1, WIDE - HALF_B1)
-    ka[0].wait_recv()
-    join_a(xo)
-    ra1 = go(ga(xo, GA1), RA.at[0, :, :, A1], dxr)
-    ra2 = go(ga(xo, GA2), RA.at[0, :, :, A2], dxl)
-    kb[0].wait_recv()
-    join_b(zo)
-    rb1 = go(gb(zo, GB1), RB.at[0, :, :, B1], dzr)
-    rb2 = go(gb(zo, GB2), RB.at[0, :, :, B2], dzl)
-    for copy in hz:
-        copy.wait_recv()
-    HX[x] = HZ[0] + HZ[1] + HZ[2] + HZ[3]
-    hx = [go(HX.at[x], HX.at[x], d) for d in (dxr, dxl, dxo)]
-    ka[1].wait_recv()
-    join_a(xr)
-    kb[1].wait_recv()
-    join_b(zr)
-    ka[2].wait_recv()
-    join_a(xl)
-    kb[2].wait_recv()
-    join_b(zl)
-
-    ra1.wait_recv()
-    G[xr, c, :, :, GA1] = add(G[xr, c, :, :, GA1], RA[0, :, :, A1]).astype(BF16)
-    sa_r = go(ga(xr, A), SA.at[0], dxr)
-    rb1.wait_recv()
-    G[:, c, zr, :, GB1] = add(G[:, c, zr, :, GB1], RB[0, :, :, B1]).astype(BF16)
-    sb_r = go(gb(zr, B), SB.at[0], dzr)
-    ra2.wait_recv()
-    G[xl, c, :, :, GA2] = add(G[xl, c, :, :, GA2], RA[0, :, :, A2]).astype(BF16)
-    sa_l = go(ga(xl, A), SA.at[1], dxl)
-    rb2.wait_recv()
-    G[:, c, zl, :, GB2] = add(G[:, c, zl, :, GB2], RB[0, :, :, B2]).astype(BF16)
-    sb_l = go(gb(zl, B), SB.at[1], dzl)
-    ka[3].wait_recv()
-    kb[3].wait_recv()
-
-    for copy in hx:
-        copy.wait_recv()
-    HC[c] = HX[0] + HX[1] + HX[2] + HX[3]
-    hc = go(HC.at[c], HC.at[c], dco)
-    load_n.wait()
-    n1.wait_recv()
-    N[yr, H1] = add(N[yr, H1], M[0]).astype(BF16)
-    n3 = go(N.at[yr], Q.at[0], dyr)
-    n2.wait_recv()
-    N[yl, H2] = add(N[yl, H2], M[1]).astype(BF16)
-    n4 = go(N.at[yl], Q.at[1], dyl)
-
-    hc.wait_recv()
-    HY[y] = HC[0] + HC[1]
-    hout_ref[...] = HY[y]
-    hy = [go(HY.at[y], HY.at[y], d) for d in (dyr, dyl, dyo)]
-
-    sa_r.wait_recv()
-    sa_l.wait_recv()
-    own = add(G[x, c, :, :, A], K[x, :, :, A]) + add(SA[0], SA[1])
-    TA[...] = own.astype(BF16)
-    ta1 = go(TA.at[zo, :, A1], UA.at[:, A1], dzr)
-    ta2 = go(TA.at[zo, :, A2], UA.at[:, A2], dzl)
-    sb_r.wait_recv()
-    sb_l.wait_recv()
-    own = add(G[:, c, z, :, B], K[:, z, :, B]) + add(SB[0], SB[1])
-    TB[...] = own.astype(BF16)
-    tb1 = go(TB.at[xo, :, B1], UB.at[:, B1], dxr)
-    tb2 = go(TB.at[xo, :, B2], UB.at[:, B2], dxl)
-    ta1.wait_recv()
-    TA[zr, :, A1] = add(TA[zr, :, A1], UA[:, A1]).astype(BF16)
-    va_r = go(TA.at[zr], VA.at[0], dzr)
-    ta2.wait_recv()
-    TA[zl, :, A2] = add(TA[zl, :, A2], UA[:, A2]).astype(BF16)
-    va_l = go(TA.at[zl], VA.at[1], dzl)
-    tb1.wait_recv()
-    TB[xr, :, B1] = add(TB[xr, :, B1], UB[:, B1]).astype(BF16)
-    vb_r = go(TB.at[xr], VB.at[0], dxr)
-    tb2.wait_recv()
-    TB[xl, :, B2] = add(TB[xl, :, B2], UB[:, B2]).astype(BF16)
-    vb_l = go(TB.at[xl], VB.at[1], dxl)
-    vb_r.wait_recv()
-    vb_l.wait_recv()
-    gout_ref[:, B] = TB[x].astype(F32) + add(VB[0], VB[1])
-    Y[y] = gout_ref[:, C_BC:C_MISC]
-    ys = [go(Y.at[y], Y.at[y], d) for d in (dyr, dyl, dyo)]
-    va_r.wait_recv()
-    va_l.wait_recv()
-    gout_ref[:, A] = TA[z].astype(F32) + add(VA[0], VA[1])
-    for copy in hy:
-        copy.wait_recv()
-    hyout_ref[...] = HY[0] + HY[1] + HY[2] + HY[3]
-    n3.wait_recv()
-    n4.wait_recv()
-    nout_ref[...] = N[y].astype(F32) + add(Q[0], Q[1])
-    for copy in ys:
-        copy.wait_recv()
-    yout_ref[...] = Y[0] + Y[1] + Y[2] + Y[3]
-    go.finish()
-
-
-def reduce_all(g, n, h):
-    nA, nB = HALF_A, WIDE - HALF_A
-    return pl.pallas_call(
-        reduce_kernel,
-        out_shape=(shape((48, WIDE), F32), shape((256, D), F32), shape((48, C_MISC - C_BC), F32), shape((64, 128), F32), shape((64, 128), F32)),
-        in_specs=[pl.BlockSpec(memory_space=ANY)] * 2 + [pl.BlockSpec(memory_space=pltpu.VMEM)],
-        out_specs=[pl.BlockSpec(memory_space=pltpu.VMEM)] * 5,
-        scratch_shapes=[
-            pltpu.VMEM((4, 2, 4, 48, WIDE), BF16), pltpu.VMEM((4, 4, 48, WIDE), BF16),
-            pltpu.VMEM((1, 4, 48, nA), BF16), pltpu.VMEM((2, 4, 48, nA), BF16),
-            pltpu.VMEM((1, 4, 48, nB), BF16), pltpu.VMEM((2, 4, 48, nB), BF16),
-            pltpu.VMEM((4, 48, nA), BF16), pltpu.VMEM((4, 48, nB), BF16),
-            pltpu.VMEM((48, nA), BF16), pltpu.VMEM((48, nB), BF16),
-            pltpu.VMEM((2, 48, nA), BF16), pltpu.VMEM((2, 48, nB), BF16),
-            pltpu.VMEM((4, 256, D), BF16), pltpu.VMEM((2, 128, D), BF16), pltpu.VMEM((2, 256, D), BF16),
-            pltpu.VMEM((4, 48, C_MISC - C_BC), F32),
-            pltpu.VMEM((4, 64, 128), F32), pltpu.VMEM((4, 64, 128), F32), pltpu.VMEM((2, 64, 128), F32),
-            pltpu.VMEM((4, 64, 128), F32),
-        ] + sems(48),
-        compiler_params=comm_params(5, 56 << 20),
-        name="reduce_all",
-    )(g, n, h)
+        finish_kernel,
+        out_shape=(
+            shape((256, D), BF16), shape((256, D), F32), shape((48, HD), F32), shape((48, HD), F32), shape((HD, 48), F32),
+            shape((48, 2 * NS), F32),
+        ),
+        in_specs=[pl.BlockSpec(memory_space=pltpu.VMEM)] * 8,
+        out_specs=[pl.BlockSpec(memory_space=pltpu.VMEM)] * 6,
+        compiler_params=pltpu.CompilerParams(vmem_limit_bytes=40 << 20),
+        name="finish",
+    )(rows, cot, out, share, gain, mid, tail, ysum)
 
 
 def after(value, *others):
@@ -1050,41 +1225,13 @@
     mixed, db, sums, entered = scan(xbc, xdt, cum, fresh, gate, pos, summs, cot_all, W, skip, gain)
     sums = swap(sums, "tp", 2, "swap_sums")
     branch, dgate, dmix, out, gfresh, gsumm, tgrad = turn(sums, mixed, gate, db, xbc, cum, pos, W, gain)
-    out = out.reshape(4, 256, D)
-    out_parts = [lax.dynamic_index_in_dim(out, tp, 0, False)] + [
-        lax.ppermute(
-            lax.dynamic_index_in_dim(out, (tp + k) % 4, 0, False), "tp", [(j, (j + k) % 4) for j in range(4)]
-        )
-        for k in (1, 3, 2)
-    ]
-    gsumms = swap(gsumm, "ctx", 3, "swap_grad")
-    din, cgrad, hgrad, dedge = back(
-        xbc, xdt, dt, cum, sig, dmix, entered, gfresh, ds, ci, pos, gsumms, edge, conv, step, skip
+    din, cgrad, hgrad, dedge, gmid, out_share = middle(
+        gsumm, out.reshape(4, 256, D), cot_all, normed, branch, dgate,
+        xbc, xdt, dt, cum, sig, dmix, entered, gfresh, ds, ci, pos, edge, conv, step, skip,
     )
-    dedge, *out_parts = lax.optimization_barrier((dedge, *out_parts))
-    dedge = edge_back(dedge, 4)
-    ngrad, din, nggrad = rows_grad(dgate, din, dedge, W, X)
-
-    cg = jnp.sum(cgrad.reshape(5, 8, CONV), axis=1)
-    tg = jnp.sum(tgrad.reshape(2, 8, HD), axis=1)
-    hg = jnp.sum(hgrad.reshape(2, 8, 128), axis=1)
-    heads = jnp.stack([hg[0, :HEADS] * rate, hg[1, :HEADS], tg[1].reshape(HEADS, 64).sum(axis=1)])
-    heads = jnp.pad(heads, ((0, 3), (0, 128 - HEADS)))
-    small = jnp.concatenate(
-        [cg.reshape(40, 128), tg[0].reshape(6, 128), jnp.sum(nggrad, axis=0).reshape(12, 128), heads], axis=0
-    )
-    wgrad = weights_grad(cot_all, normed, branch, dgate, din)
-    gsum, share, ysum, plane, every = reduce_all(wgrad.reshape(4, 2, 4, 48, WIDE), ngrad.reshape(4, 256, D), small)
-
-    own = layer_input.astype(F32)
-    out_share = sum(part.astype(F32) for part in out_parts)
-    layer_output = (own + out_share).astype(BF16)
-    scale = lax.rsqrt(jnp.mean(own * own, axis=1, keepdims=True) + EPS)
-    weighted = share * ngain
-    input_grad = (
-        scale * weighted
-        - own * (scale * scale * scale) * jnp.mean(own * weighted, axis=1, keepdims=True)
-        + out_cotangent.astype(F32)
+    gtail, share, ysum, plane, every = tail(dgate, din, W, X, normed, dedge, cgrad, tgrad, hgrad)
+    layer_output, input_grad, d_gate, d_input, d_out, d_state = finish(
+        layer_input, out_cotangent, out_share, share, ngain, gmid, gtail, ysum
     )
     block = lax.axis_index("shard") * 4 + ctx
     conv_sum = plane[:40].reshape(5, CONV)[:, :HD].reshape(5, HEADS, 64)
@@ -1095,19 +1242,19 @@
         layer_output,
         input_grad,
         lax.dynamic_slice_in_dim(every[46:58].reshape(D), block * 48 + tp * 12, 12, 0),
-        gsum[:, C_GATE:C_IN],
-        gsum[:, C_IN:C_BC],
-        gsum[:, C_MISC : C_MISC + HEADS],
-        lax.dynamic_slice_in_dim(ysum, tp * 12, 12, 0),
+        d_gate,
+        d_input,
+        gtail[:, CONV : CONV + HEADS],
+        lax.dynamic_slice_in_dim(d_state, tp * 12, 12, 0),
         conv_sum[:4],
         conv_sum[4],
         state_sum[:4],
         state_sum[4],
-        plane[58, :HEADS],
-        plane[59, :HEADS],
-        plane[60, :HEADS],
+        plane[64, :HEADS] * rate,
+        plane[65, :HEADS],
+        plane[58:64].reshape(HEADS, 64).sum(axis=1),
         gain_sum,
-        gsum[:, C_OUT:C_GATE].T,
+        d_out,
     )
 
 

time: 284 us -> 260 us (0.915)
  Pallas kernels: 222 us -> 210 us
  other arithmetic: 11.3 us -> 3.45 us
  local copies, waits for them, and re-layouts: 35.5 us -> 39.7 us
  starting transfers between devices: 9.12 us -> 5.03 us
  waiting for transfers between devices: 3.08 us -> 0.01 us
    pallas_call x3 -> x2, Pallas kernels: 28.8 us -> 18.3 us  [swap(): pl.pallas_call(functools.partial(swap_kernel, axis), out_shape=shape((4,)...]
    unnamed x35 -> x41, local copies, waits for them, and re-layouts: 8.04 us -> 14.7 us
    reduce_sum x6 -> x1, other arithmetic: 5.23 us -> 0.63 us  [per_device(): plane[58:64].reshape(HEADS, 64).sum(axis=1)]
    ppermute x3 -> x0, starting transfers between devices: 4.08 us -> none  [per_device(): lax.ppermute(lax.dynamic_index_in_dim(out, (tp + k) % 4, 0, False), 'tp',...]
    add x1 -> x0, other arithmetic: 3.9 us -> none  [per_device(): scale * weighted]
    squeeze x2 -> x1, local copies, waits for them, and re-layouts: 4.62 us -> 1.19 us  [per_device(): plane[65, :HEADS]]
    ppermute x3 -> x0, waiting for transfers between devices: 3.07 us -> none  [per_device(): lax.ppermute(lax.dynamic_index_in_dim(out, (tp + k) % 4, 0, False), 'tp',...]
    pallas_call x5 -> x3, Pallas kernels: 102 us -> 100 us  [the longest x1 50 us: tail(): pl.pallas_call(tail_kernel, out_shape=(shape((48, CONV + 128), F32), shap...]
  transfers between devices with their start and end apart: 6 -> 3, of which waited for: 2 -> 0; matrix products, arithmetic and copies ran while one was open for 5% -> 4% of each run, Pallas kernels for 21% -> 13%
where the time goes in v2:
time: 260 us; the launch traced here: 259 us
  Pallas kernels  210 us (81%)
  local copies, waits for them, and re-layouts  39.7 us (15%)
  starting transfers between devices  5.03 us (2%)
  other arithmetic  3.45 us (1%)
    pallas_call x1, Pallas kernels, tail(): pl.pallas_call(tail_kernel, out_shape=(shape((48, CONV + 128), F32), shap...  50 us
    pallas_call x1, Pallas kernels, middle(): pl.pallas_call(middle_kernel, grid=(PRE + CHUNKS,), in_specs=[anywhere, a...  48.2 us
    pallas_call x1, Pallas kernels, gather(): pl.pallas_call(gather_kernel, out_shape=(shape((4, 2, 4, 48, WIDE), BF16)...  43.1 us
    pallas_call x1, Pallas kernels, front(): pl.pallas_call(front_kernel, grid=(ROWS // tile,), in_specs=[rows_spec(ti...  21.9 us
    pallas_call x2, Pallas kernels, swap(): pl.pallas_call(functools.partial(swap_kernel, axis), out_shape=shape((4,)...  18.3 us
    unnamed x41, local copies, waits for them, and re-layouts  14.7 us
    pallas_call x1, Pallas kernels, turn(): pl.pallas_call(turn_kernel, grid=(ROWS // tile,), in_specs=[pl.BlockSpec(...  13.6 us
    pallas_call x1, Pallas kernels, scan(): pl.pallas_call(scan_kernel, grid=(ROWS // tile,), in_specs=[rows_spec(til...  12.7 us
  transfers between devices with their start and end apart: 3, of which 0 were waited for; matrix products, arithmetic and copies ran while one was open for 4% of the time, Pallas kernels for 13%

profile of v2, /device:TPU:0, one launch (start us, length us, event | category | flops | bytes accessed | tf_op | source)
XLA Modules:
  0.0 258.9 jit_solution(14357489283068650058)
XLA Ops:
  0.6 0.7 copy.67
  1.4 0.8 copy.68
  2.2 0.7 copy.66
  3.1 0.8 copy.69
  3.9 0.8 copy.71
  4.6 0.7 pad.21
  5.3 0.7 pad.22
  6.0 1.8 concatenate.12.w_ref
  7.7 43.1 %gather_weights.1 = (bf16[4,2,4,48,2688]{4,3,2,1,0:T(8,128)(2,1)}, bf16[4,256,1536]{2,1,0:T(8,128)(2,1)}, bf16[16,1536]{1,0:T(8,128)(2,1)}) custom-call(bf16[48,2688]{1,0:T(8,128)(2,1)} %concatenate.12.w_ref, bf16[256,1536]{1,0:T(8,128)(2,1)} %x_ref.3), custom_call_target="tpu_custom_call" | custom-call | tf_op jit(solution)/shard_map/gather_weights/pallas_call | solution.py:225
  50.8 1.4 collective-permute-start
  52.2 1.9 collective-permute-start.1
  54.1 1.7 collective-permute-start.2
  55.8 1.0 slice.84
  59.1 0.7 reshape_squeeze.3.gain_ref
  60.8 0.7 maximum_maximum_fusion.conv_ref
  61.5 1.0 broadcast_in_dim.54.pos_ref
  62.5 21.9 %front.1 = (bf16[1024,1536]{1,0:T(8,128)(2,1)}, f32[1024,768]{1,0:T(8,128)}, bf16[1024,1024]{1,0:T(8,128)(2,1)}, bf16[16,1024]{1,0:T(8,128)(2,1)}, f32[1024,1024...) custom-call(bf16[1024,1536]{1,0:T(8,128)(2,1)} %bitcast.62, ...), custom_call_target="tpu_custom_call" | custom-call | flops 6039797760 | bytes 41943040 | tf_op jit(solution)/shard_map/front/pallas_call | solution.py:417
  84.3 12.0 %swap_state.1.summ_ref = bf16[4,144,768]{2,1,0:T(8,128)(2,1)} custom-call(bf16[144,768]{1,0:T(8,128)(2,1)} %get-tuple-element.68.own_ref), custom_call_target="tpu_custom_call" | custom-call | tf_op jit(solution)/shard_map/swap_state/pallas_call | solution.py:263
  96.4 0.8 reshape_reshape.11.gain_ref
  97.2 0.7 broadcast_in_dim_reshape.3.skip_ref
  98.2 1.2 bitcast_dynamic-update-slice_fusion.2
  99.4 1.2 bitcast_dynamic-update-slice_fusion.1
  100.7 1.7 copy-done.9
  102.4 12.7 %scan.1 = (f32[1024,768]{1,0:T(8,128)}, f32[1024,768]{1,0:T(8,128)}, f32[64,128]{1,0:T(8,128)}, bf16[8,128,768]{2,1,0:T(8,128)(2,1)}) custom-call(bf16[1024,1024]{1,0:T(8,128)(2,1)} %get-tuple-element.63.xbc_ref, bf16[1024,768]{1,0:T(8,128)(2,1)} %get-tuple-element.64.xdt_ref, f32[1024,128]{1,0:T(8,128)} %get-tuple-element.65.cum_ref, ...), custom_call_target="tpu_custom_call" | custom-call | flops 2831155200 | bytes 31457280 | tf_op jit(solution)/shard_map/scan/pallas_call | solution.py:500
  115.0 6.3 %swap_sums.1.sums_ref = f32[4,64,128]{2,1,0:T(8,128)} custom-call(f32[64,128]{1,0:T(8,128)} %get-tuple-element.70.own_ref), custom_call_target="tpu_custom_call" | custom-call | tf_op jit(solution)/shard_map/swap_sums/pallas_call | solution.py:263
  121.3 13.6 %turn.1 = (bf16[1024,768]{1,0:T(8,128)(2,1)}, bf16[1024,768]{1,0:T(8,128)(2,1)}, f32[1024,768]{1,0:T(8,128)}, bf16[1024,1536]{1,0:T(8,128)(2,1)}, f32[8,128,768]...) custom-call(f32[4,64,128]{2,1,0:T(8,128)} %swap_sums.1.sums_ref, f32[1024,768]{1,0:T(8,128)} %get-tuple-element.71.mixed_ref, ...), custom_call_target="tpu_custom_call" | custom-call | flops 2831155200 | bytes 31457280 | tf_op jit(solution)/shard_map/turn/pallas_call | solution.py:581
  135.0 48.2 %middle.1 = (bf16[1024,1152]{1,0:T(8,128)(2,1)}, f32[40,1024]{1,0:T(8,128)}, f32[16,128]{1,0:T(8,128)}, f32[8,1024]{1,0:T(8,128)}, f32[48,1536]{1,0:T(8,128)}, /*index=5*/f32[256,1536]{1,0:T(8,128)}) custom-call(bf16[144,768]{1,0:T(8,128)(2,1)} %get-tuple-element.73.gsumm_ref, bf16[4,256,1536]{2,1,0:T(8,128)(2,1)} %bitcast.65, bf16[1024,1536]{1,0:T(8,128)(2,1)} %bitcast.56, ...), custom_call_target="tpu_custom_call" | custom-call | flops 4026531840 | bytes 31457280 | tf_op jit(solution)/shard_map/middle/pallas_call | solution.py:990
  183.2 50.0 %tail.1 = (f32[48,1152]{1,0:T(8,128)}, f32[256,1536]{1,0:T(8,128)}, f32[48,256]{1,0:T(8,128)}, f32[72,128]{1,0:T(8,128)}, f32[72,128]{1,0:T(8,128)}) custom-call(bf16[1024,768]{1,0:T(8,128)(2,1)} %get-tuple-element.77.dgate_ref, bf16[1024,1152]{1,0:T(8,128)(2,1)} %get-tuple-element.87.din_ref, bf16[1536,2688]{1,0:T(8,128)(2,1)} %bitcast.54, ...), custom_call_target="tpu_custom_call" | custom-call | tf_op jit(solution)/shard_map/tail/pallas_call | solution.py:1115
  233.2 0.7 slice.76
  235.2 1.3 slice.72
  236.5 0.7 fusion.2
  237.2 1.3 slice_bitcast_fusion
  238.5 1.2 bitcast_multiply_fusion
  239.7 1.2 slice_bitcast_fusion.1
  240.9 1.4 slice.71
  242.2 1.4 copy-done.3
  243.6 1.0 copy-done.4
  244.6 0.9 copy-done.5
  245.5 0.8 copy-done.6
  246.3 1.9 finish.1
  248.9 0.8 copy.83
  249.7 0.7 reshape.114
  250.6 0.7 copy.82
  251.4 0.7 copy.78
  252.0 1.3 copy.92
  254.1 1.4 copy.81
  256.2 1.3 constant_dynamic-slice_fusion.4
  257.6 1.3 dynamic_slice.15
  (71 shorter events, 7.4 us)
Async XLA Ops:
  50.8 47.4 %collective-permute-start = (bf16[256,1536]{1,0:T(8,128)(2,1)}, bf16[256,1536]{1,0:T(8,128)(2,1)}, u32[]{:S(2)}, u32[]{:S(2)}) collective-permute-start(bf16[256,1536]{1,0:T(8,128)(2,1)} %cot_ref.1), channel_id=1, source_target_pairs={{0,1},{1,2},{2,3},{3,0},{4,5},{5,6},{6,7},{7,4},{8,9},{9,10},{10,1... | collective-permute-start | bytes 2359304 | tf_op jit(solution)/shard_map/ppermute | solution.py:1205
  52.2 47.2 %collective-permute-start.1 = (bf16[256,1536]{1,0:T(8,128)(2,1)}, bf16[256,1536]{1,0:T(8,128)(2,1)}, u32[]{:S(2)}, u32[]{:S(2)}) collective-permute-start(bf16[256,1536]{1,0:T(8,128)(2,1)} %cot_ref.1), channel_id=1, source_target_pairs={{0,3},{1,0},{2,1},{3,2},{4,7},{5,4},{6,5},{7,6},{8,11},{9,8},{10,9... | collective-permute-start | bytes 2359304 | tf_op jit(solution)/shard_map/ppermute | solution.py:1205
  54.1 46.5 %collective-permute-start.2 = (bf16[256,1536]{1,0:T(8,128)(2,1)}, bf16[256,1536]{1,0:T(8,128)(2,1)S(1)}, u32[]{:S(2)}, u32[]{:S(2)}) collective-permute-start(bf16[256,1536]{1,0:T(8,128)(2,1)} %cot_ref.1), channel_id=1, source_target_pairs={{0,2},{1,3},{2,0},{3,1},{4,6},{5,7},{6,4},{7,5},{8,10},{9,11},{10,... | collective-permute-start | bytes 2359304 | tf_op jit(solution)/shard_map/ppermute | solution.py:1205
  57.0 2.8 %copy-start.12 = (s32[1,4]{1,0:T(1,128)S(1)}, s32[1,4]{1,0:T(1,128)}, u32[]{:S(2)}) copy-start(s32[1,4]{1,0:T(1,128)} %param.19) | copy-start | bytes 52
  57.0 3.0 %copy-start.13 = (f32[12]{0:T(128)S(1)}, f32[12]{0:T(128)}, u32[]{:S(2)}) copy-start(f32[12]{0:T(128)} %param.29) | copy-start | bytes 148
  57.0 3.1 %copy-start.11 = (f32[12]{0:T(128)S(1)}, f32[12]{0:T(128)}, u32[]{:S(2)}) copy-start(f32[12]{0:T(128)} %param.30) | copy-start | bytes 148
  62.5 34.7 %copy-start.10 = (f32[12]{0:T(128)S(1)}, f32[12]{0:T(128)}, u32[]{:S(2)}) copy-start(f32[12]{0:T(128)} %param.31) | copy-start | bytes 148
  84.3 13.8 %copy-start = (bf16[256,1536]{1,0:T(8,128)(2,1)S(1)}, bf16[256,1536]{1,0:T(8,128)(2,1)}, u32[]{:S(2)}) copy-start(bf16[256,1536]{1,0:T(8,128)(2,1)} %cot_ref.1) | copy-start | bytes 2359300
  100.7 1.7 copy-start.9
  183.2 59.0 %copy-start.1 = (bf16[256,1536]{1,0:T(8,128)(2,1)S(1)}, bf16[256,1536]{1,0:T(8,128)(2,1)}, u32[]{:S(2)}) copy-start(bf16[256,1536]{1,0:T(8,128)(2,1)} %x_ref.3) | copy-start | bytes 2359300
  183.2 59.0 %copy-start.2 = (f32[256,1536]{1,0:T(8,128)S(1)}, f32[256,1536]{1,0:T(8,128)}, u32[]{:S(2)}) copy-start(f32[256,1536]{1,0:T(8,128)} %get-tuple-element.86.out_ref) | copy-start | bytes 4718596
  183.2 59.0 %copy-start.7 = (f32[1,1536]{1,0:T(1,128)S(1)}, f32[1,1536]{1,0:T(1,128)}, u32[]{:S(2)}) copy-start(f32[1,1536]{1,0:T(1,128)} %reshape_squeeze.3.gain_ref) | copy-start | bytes 18436
  242.2 1.4 copy-start.3
  243.6 1.0 copy-start.4
  244.6 0.9 copy-start.5
  245.5 0.8 copy-start.6
  248.3 0.6 copy-start.8
